TPU v7x, 128 devices: a whole 4x4x4 slice. The times are simulated.
128 devices in a mesh: blk: 128 (over z, x, y, core).
Axes of the slice: x: 4, y: 4, z: 4, core: 2. Of those that a mesh axis runs over, the one named last changes fastest.
Arguments:
- fitted_tensor: bfloat16 [384, 3, 256, 2048], P('blk'), may hold values from -0.125 to 0.125
- block_slot: int32 [256], replicated, may hold values from 0 to 383, as said below
- pair_list: int32 [6144, 2], replicated, may hold values from 0 to 255, as said below
- domain_slots: int32 [6144, 4], replicated, may hold values from 0 to 2
Outputs:
- exchange: float32 [384, 256, 256], P('blk')
Inputs may be any that keep to these rules, and one draw needn't show every extreme that they name: `block_slot`: slots rise with block numbers. The blocks owned by device d fill its first slots d * 3, d * 3 + 1, ...; every device owns 1 to 3 blocks, devices 2j and 2j + 1 own 2 * 2 together, and some device owns 3. `pair_list`: each row (a, b) has a < b <= a + 2; some row reaches b = a + 2 with the owners 2 devices apart.
All inputs are finite; a program needn't handle non-finite values.
Results may differ from a plain program's by a relative error of at most 0.0003.
Values may be sent and summed in bfloat16 or wider, within the bound.
No kernel may reach another device: no remote copies, remote signals or barrier semaphores. Data moves between devices by JAX's collectives and lax.ppermute only.
A program may use at most 256 MiB of HBM per device.

v0:
```python
import jax
import jax.numpy as jnp
from jax import lax
from jax.sharding import PartitionSpec as P

REACH = 2


def from_behind(value, axis, steps):
    count = lax.axis_size(axis)
    leading, last = (max(0, -steps), min(count, count - steps))
    return lax.ppermute(value, axis, [(source, source + steps) for source in range(leading, last)])


def per_device(fitted_tensor, block_slot, pair_list, domain_slots):
    own_cap = fitted_tensor.shape[0]
    aux_count = fitted_tensor.shape[1]
    half_width = domain_slots.shape[1] // 2
    this_device = lax.axis_index("blk")
    owners = block_slot // own_cap
    local_slot = block_slot % own_cap
    live_blocks = jnp.sum((owners == this_device).astype(jnp.int32))
    slot_range = jnp.arange(own_cap, dtype=jnp.int32)
    aux_range = jnp.arange(aux_count, dtype=jnp.int32)
    live_mask = (slot_range < live_blocks).astype(jnp.float32)
    diag_sum = jnp.einsum(
        "skbx,skcx->sbc", fitted_tensor, fitted_tensor, preferred_element_type=jnp.float32
    )
    exchange_sum = diag_sum * live_mask[:, None, None]
    first_block = pair_list[:, 0]
    second_block = pair_list[:, 1]
    owner_first = owners[first_block]
    distance = owners[second_block] - owner_first
    slot_first = local_slot[first_block]
    slot_second = local_slot[second_block]
    mine = owner_first == this_device
    second_hot = (slot_second[:, None] == slot_range[None, :]).astype(jnp.float32)
    left_aux = (domain_slots[:, :half_width, None] == aux_range[None, None, :]).astype(jnp.float32)
    right_aux = (domain_slots[:, half_width:, None] == aux_range[None, None, :]).astype(jnp.float32)
    aux_pairs = jnp.einsum("pjk,pjl->pkl", left_aux, right_aux)
    own_wide = fitted_tensor.astype(jnp.float32)
    weighted = None
    for reach_step in range(REACH + 1):
        chosen = (mine & (distance == reach_step)).astype(jnp.float32)
        first_hot = (slot_first[:, None] == slot_range[None, :]).astype(jnp.float32) * chosen[
            :, None
        ]
        counts = jnp.einsum("pa,pb,pkl->abkl", first_hot, second_hot, aux_pairs)
        if reach_step == 0:
            source = fitted_tensor
        else:
            source = from_behind(fitted_tensor, "blk", -reach_step)
        sent_slots = source.shape[0]
        counts_bf = counts.astype(jnp.bfloat16)
        part_sum = jnp.einsum(
            "abkl,blix->akix", counts_bf, source, preferred_element_type=jnp.float32
        )
        weighted = part_sum if weighted is None else weighted + part_sum
        right_sum = jnp.einsum(
            "abkl,akix->blix", counts_bf, fitted_tensor, preferred_element_type=jnp.float32
        )
        flipped = jnp.einsum(
            "blyx,blix->byi", source.astype(jnp.float32), right_sum, precision=lax.Precision.HIGHEST
        )
        if reach_step == 0:
            exchange_sum = exchange_sum + flipped
        else:
            returned_back = from_behind(flipped, "blk", reach_step)
            exchange_sum = exchange_sum.at[:sent_slots].add(returned_back)
    own_part = jnp.einsum("akix,akjx->aij", own_wide, weighted, precision=lax.Precision.HIGHEST)
    return exchange_sum + own_part


def solution(mesh):
    placed = (P("blk", None, None, None), P(), P(), P())
    return jax.shard_map(
        per_device, mesh=mesh, in_specs=placed, out_specs=P("blk", None, None), check_vma=False
    )
```

profile of v0, /device:TPU:63, one launch (start us, length us, event | category | flops | bytes accessed | tf_op | source)
XLA Modules:
  0.0 512.2 jit_solution(1080042377010015039)
XLA Ops:
  0.0 2.4 collective-permute-start.2
  2.4 2.9 collective-permute-start
  6.2 1.3 fusion.70
  7.6 38.3 %gather_fusion.3 = s32[6144]{0:T(1024)S(1)} fusion(s32[256]{0:T(256)S(1)} %get-tuple-element.46, s32[6144]{0:T(1024)S(1)} %broadcast_clamp_fusion.1), kind=kCustom, calls=%fused_computation.3 | custom fusion | bytes 73728 | tf_op jit(solution)/shard_map/gather | solution.py:33
  45.9 38.4 %gather_fusion = s32[6144]{0:T(1024)S(1)} fusion(s32[256]{0:T(256)S(1)} %get-tuple-element.58, s32[6144]{0:T(1024)S(1)} %broadcast_clamp_fusion.1), kind=kCustom, calls=%fused_computation | custom fusion | bytes 73728 | tf_op jit(solution)/shard_map/gather | solution.py:35
  84.3 38.4 %gather_fusion.2 = s32[6144]{0:T(1024)S(1)} fusion(s32[256]{0:T(256)S(1)} %get-tuple-element.46, s32[6144]{0:T(1024)S(1)} %broadcast_clamp_fusion), kind=kCustom, calls=%fused_computation.2 | custom fusion | bytes 73728 | tf_op jit(solution)/shard_map/gather | solution.py:32
  122.6 38.4 %gather_fusion.1 = s32[6144]{0:T(1024)S(1)} fusion(s32[256]{0:T(256)S(1)} %get-tuple-element.58, s32[6144]{0:T(1024)S(1)} %broadcast_clamp_fusion), kind=kCustom, calls=%fused_computation.1 | custom fusion | bytes 73728 | tf_op jit(solution)/shard_map/gather | solution.py:34
  162.2 2.2 copy.15
  164.4 51.7 %fusion.20 = bf16[6144,3,3]{2,1,0:T(4,128)(2,1)} fusion(s32[6144,2]{1,0:T(8,128)} %copy.15, s32[6144,2]{1,0:T(8,128)S(1)} %copy.14), kind=kOutput, calls=%fused_computation.26 | convolution fusion | flops 294912 | bytes 208896 | tf_op jit(solution)/shard_map/pjk,pjl->pkl/dot_general | solution.py:40
  216.2 7.9 %copy.16 = bf16[6144,3,3]{0,2,1:T(4,128)(2,1)S(1)} copy(bf16[6144,3,3]{2,1,0:T(4,128)(2,1)} %fusion.20) | data formatting | bytes 221184 | tf_op jit(solution)/shard_map/pjk,pjl->pkl/dot_general | solution.py:40
  225.0 22.1 %fusion.27 = f32[3,3,256,2048,1]{3,1,4,2,0:T(4,128)} fusion(bf16[3,3,256,2048,1]{3,2,1,0,4:T(8,128)(2,1)} %bitcast.122, bf16[3,3,3,3]{3,1,2,0:T(4,128)(2,1)S(1)} %convolution_convert_fusion.2), kind=kOutput, calls=%fused_computation.33 | convolution fusion | flops 84934656 | bytes 28311714 | tf_op jit(solution)/shard_map/abkl,akix->blix/dot_general | solution.py:59
  249.3 28.2 %fusion.33 = f32[3,256,256]{2,1,0:T(8,128)} fusion(bf16[3,3,256,2048]{3,2,1,0:T(8,128)(2,1)S(1)} %bitcast.125, f32[3,3,256,2048,1]{3,1,4,2,0:T(4,128)} %fusion.27), kind=kOutput, calls=%fused_computation.39 | convolution fusion | flops 14495514624 | bytes 29097984 | tf_op jit(solution)/shard_map/blyx,blix->byi/dot_general | solution.py:62
  277.5 9.3 %fusion.44 = f32[3,256,256]{2,1,0:T(8,128)S(1)} fusion(f32[3,256,256]{2,1,0:T(8,128)} %fusion.33, bf16[3,3,256,2048]{3,2,1,0:T(8,128)(2,1)} %param.12, f32[3]{0:T(128)S(1)} %compare_convert_fusion), kind=kOutput, calls=%fused_computation.45 | convolution fusion | flops 2416312320 | bytes 11010060 | tf_op jit(solution)/shard_map/skbx,skcx->sbc/dot_general | solution.py:26
  286.9 22.1 %fusion.25 = f32[3,3,256,2048,1]{3,1,4,2,0:T(4,128)} fusion(bf16[3,3,256,2048,1]{3,2,1,0,4:T(8,128)(2,1)} %bitcast.123, bf16[3,3,3,3]{3,1,2,0:T(4,128)(2,1)S(1)} %convolution_convert_fusion.1), kind=kOutput, calls=%fused_computation.31 | convolution fusion | flops 84934656 | bytes 28311714 | tf_op jit(solution)/shard_map/abkl,akix->blix/dot_general | solution.py:59
  309.0 17.8 %fusion.23 = f32[3,3,256,2048,1]{3,1,4,2,0:T(4,128)} fusion(bf16[3,3,256,2048,1]{3,2,1,0,4:T(8,128)(2,1)S(1)} %bitcast.128, bf16[3,3,3,3]{3,1,2,0:T(4,128)(2,1)S(1)} %convolution_convert_fusion), kind=kOutput, calls=%fused_computation.29 | convolution fusion | flops 84934656 | bytes 28311714 | tf_op jit(solution)/shard_map/abkl,akix->blix/dot_general | solution.py:59
  326.8 25.2 %fusion.18 = f32[3,3,256,2048,1]{3,0,4,2,1:T(4,128)} fusion(bf16[3,3,256,2048,1]{3,2,1,0,4:T(8,128)(2,1)S(1)} %bitcast.129, bf16[3,3,3,3]{3,1,2,0:T(4,128)(2,1)S(1)} %convolution_convert_fusion.2), kind=kOutput, calls=%fused_computation.24 | convolution fusion | flops 84934656 | bytes 28311714 | tf_op jit(solution)/shard_map/abkl,blix->akix/dot_general | solution.py:55
  352.1 26.4 %fusion.36 = f32[3,256,256]{2,1,0:T(8,128)S(1)} fusion(bf16[3,3,256,2048]{3,2,1,0:T(8,128)(2,1)} %collective-permute-done, f32[3,3,256,2048,1]{3,1,4,2,0:T(4,128)} %fusion.25), kind=kOutput, calls=%fused_computation.40 | convolution fusion | flops 14495514624 | bytes 29097984 | tf_op jit(solution)/shard_map/blyx,blix->byi/dot_general | solution.py:62
  378.5 7.0 %collective-permute-start.1 = (f32[3,256,256]{2,1,0:T(8,128)S(1)}, f32[3,256,256]{2,1,0:T(8,128)S(1)}, u32[]{:S(2)}, u32[]{:S(2)}) collective-permute-start(f32[3,256,256]{2,1,0:T(8,128)S(1)} %fusion.36), channel_id=1, source_target_pairs={{0,1},{1,2},{2,3},{3,4},{4,5},{5,6},{6,7},{7,8},{8,9},{9,10},{10,1... | collective-permute-start | bytes 2359304 | tf_op jit(solution)/shard_map/ppermute | solution.py:12
  385.6 26.7 %fusion.16 = f32[3,3,256,2048,1]{3,0,4,2,1:T(4,128)} fusion(bf16[3,3,256,2048,1]{3,2,1,0,4:T(8,128)(2,1)} %bitcast.35, bf16[3,3,3,3]{3,1,2,0:T(4,128)(2,1)S(1)} %convolution_convert_fusion.1), kind=kOutput, calls=%fused_computation.22 | convolution fusion | flops 84934656 | bytes 28311714 | tf_op jit(solution)/shard_map/abkl,blix->akix/dot_general | solution.py:55
  412.3 26.4 %fusion.14 = f32[3,3,256,2048,1]{3,0,4,2,1:T(4,128)} fusion(bf16[3,3,256,2048,1]{3,2,1,0,4:T(8,128)(2,1)} %bitcast.38, bf16[3,3,3,3]{3,1,2,0:T(4,128)(2,1)S(1)} %convolution_convert_fusion), kind=kOutput, calls=%fused_computation.20 | convolution fusion | flops 84934656 | bytes 28311714 | tf_op jit(solution)/shard_map/abkl,blix->akix/dot_general | solution.py:55
  438.6 26.5 %fusion.39 = f32[3,256,256]{2,1,0:T(8,128)S(1)} fusion(bf16[3,3,256,2048]{3,2,1,0:T(8,128)(2,1)} %collective-permute-done.2, f32[3,3,256,2048,1]{3,1,4,2,0:T(4,128)} %fusion.23), kind=kOutput, calls=%fused_computation.41 | convolution fusion | flops 14495514624 | bytes 29097984 | tf_op jit(solution)/shard_map/blyx,blix->byi/dot_general | solution.py:62
  465.2 2.8 collective-permute-start.3
  468.0 42.6 %fusion.43 = f32[3,256,256]{2,1,0:T(8,128)S(1)} fusion(bf16[3,3,256,2048]{3,2,1,0:T(8,128)(2,1)} %param.12, f32[3,3,256,2048,1]{3,0,4,2,1:T(4,128)} %fusion.14, f32[3,3,256,2048,1]{3,0,4,2,1:T(4,128)} %fusion.16, f32[3,3,256,2048,1]{3,0,4,2,1:T(4,128)} %fusion.18), kind=kOutput, calls=%fused_computation.44 | convolution fusion | flops 14504951808 | bytes 66846720 | tf_op jit(solution)/shard_map/akix,akjx->aij/dot_general | solution.py:70
  510.6 1.1 add_add_fusion
  (33 shorter events, 5.2 us)
Async XLA Ops:
  0.0 412.3 %collective-permute-start.2 = (bf16[3,3,256,2048]{3,2,1,0:T(8,128)(2,1)}, bf16[3,3,256,2048]{3,2,1,0:T(8,128)(2,1)}, u32[]{:S(2)}, u32[]{:S(2)}) collective-permute-start(bf16[3,3,256,2048]{3,2,1,0:T(8,128)(2,1)} %param.12), channel_id=1, source_target_pairs={{2,0},{3,1},{4,2},{5,3},{6,4},{7,5},{8,6},{9,7},{10,8},{11,9},{12,... | collective-permute-start | bytes 28311560 | tf_op jit(solution)/shard_map/ppermute | solution.py:12
  2.4 349.7 %collective-permute-start = (bf16[3,3,256,2048]{3,2,1,0:T(8,128)(2,1)}, bf16[3,3,256,2048]{3,2,1,0:T(8,128)(2,1)}, u32[]{:S(2)}, u32[]{:S(2)}) collective-permute-start(bf16[3,3,256,2048]{3,2,1,0:T(8,128)(2,1)} %param.12), channel_id=1, source_target_pairs={{1,0},{2,1},{3,2},{4,3},{5,4},{6,5},{7,6},{8,7},{9,8},{10,9},{11,1... | collective-permute-start | bytes 28311560 | tf_op jit(solution)/shard_map/ppermute | solution.py:12
  122.6 38.4 %copy-start = (s32[6144,4]{0,1:T(4,128)S(1)}, s32[6144,4]{0,1:T(4,128)}, u32[]{:S(2)}) copy-start(s32[6144,4]{0,1:T(4,128)} %param.15) | copy-start | bytes 294916
  216.2 33.1 %slice-start = ((s8[9437184]{0:T(1024)(128)(4,1)}), s8[1048576]{0:T(1024)(128)(4,1)S(1)}, s32[]{:S(2)}) async-start(s8[9437184]{0:T(1024)(128)(4,1)} %bitcast.124), calls=%async_computation | async-start | bytes 2097152
  225.0 24.3 %slice-start.1 = ((s8[9437184]{0:T(1024)(128)(4,1)}), s8[4194304]{0:T(1024)(128)(4,1)S(1)}, s32[]{:S(2)}) async-start(s8[9437184]{0:T(1024)(128)(4,1)} %bitcast.124), calls=%async_computation.1 | async-start | bytes 8388608
  225.0 24.3 %slice-start.2 = ((s8[9437184]{0:T(1024)(128)(4,1)}), s8[4194304]{0:T(1024)(128)(4,1)S(1)}, s32[]{:S(2)}) async-start(s8[9437184]{0:T(1024)(128)(4,1)} %bitcast.124), calls=%async_computation.2 | async-start | bytes 8388608
  277.5 31.5 %slice-start.3 = ((s8[9437184]{0:T(1024)(128)(4,1)}), s8[1048576]{0:T(1024)(128)(4,1)S(1)}, s32[]{:S(2)}) async-start(s8[9437184]{0:T(1024)(128)(4,1)} %bitcast.126), calls=%async_computation.3 | async-start | bytes 2097152
  286.9 22.1 %slice-start.4 = ((s8[9437184]{0:T(1024)(128)(4,1)}), s8[4194304]{0:T(1024)(128)(4,1)S(1)}, s32[]{:S(2)}) async-start(s8[9437184]{0:T(1024)(128)(4,1)} %bitcast.126), calls=%async_computation.4 | async-start | bytes 8388608
  286.9 22.1 %slice-start.5 = ((s8[9437184]{0:T(1024)(128)(4,1)}), s8[4194304]{0:T(1024)(128)(4,1)S(1)}, s32[]{:S(2)}) async-start(s8[9437184]{0:T(1024)(128)(4,1)} %bitcast.126), calls=%async_computation.5 | async-start | bytes 8388608
  378.5 132.0 %collective-permute-start.1 = (f32[3,256,256]{2,1,0:T(8,128)S(1)}, f32[3,256,256]{2,1,0:T(8,128)S(1)}, u32[]{:S(2)}, u32[]{:S(2)}) collective-permute-start(f32[3,256,256]{2,1,0:T(8,128)S(1)} %fusion.36), channel_id=1, source_target_pairs={{0,1},{1,2},{2,3},{3,4},{4,5},{5,6},{6,7},{7,8},{8,9},{9,10},{10,1... | collective-permute-start | bytes 2359304 | tf_op jit(solution)/shard_map/ppermute | solution.py:12
  465.2 45.4 %collective-permute-start.3 = (f32[3,256,256]{2,1,0:T(8,128)S(1)}, f32[3,256,256]{2,1,0:T(8,128)S(1)}, u32[]{:S(2)}, u32[]{:S(2)}) collective-permute-start(f32[3,256,256]{2,1,0:T(8,128)S(1)} %fusion.39), channel_id=1, source_target_pairs={{0,2},{1,3},{2,4},{3,5},{4,6},{5,7},{6,8},{7,9},{8,10},{9,11},{10,... | collective-permute-start | bytes 2359304 | tf_op jit(solution)/shard_map/ppermute | solution.py:12
where the time goes:
time: 520 us; the launch traced here: 512 us
  matrix products  327 us (63%)
  local copies, waits for them, and re-layouts  165 us (32%)
  starting transfers between devices  15.1 us (3%)
    dot_general x3, matrix products, per_device(): jnp.einsum('blyx,blix->byi', source.astype(jnp.float32), right_sum, preci...  81.2 us
    dot_general x3, matrix products, per_device(): jnp.einsum('abkl,blix->akix', counts_bf, source, preferred_element_type=j...  78.3 us
    dot_general x3, matrix products, per_device(): jnp.einsum('abkl,akix->blix', counts_bf, fitted_tensor, preferred_element...  62 us
    dot_general x1, matrix products, per_device(): aux_pairs = jnp.einsum('pjk,pjl->pkl', left_aux, right_aux)  51.7 us
    dot_general x1, matrix products, per_device(): jnp.einsum('akix,akjx->aij', own_wide, weighted, precision=lax.Precision....  42.6 us
    gather x1, local copies, waits for them, and re-layouts, per_device(): slot_second = local_slot[second_block]  38.4 us
    gather x1, local copies, waits for them, and re-layouts, per_device(): slot_first = local_slot[first_block]  38.4 us
    gather x1, local copies, waits for them, and re-layouts, per_device(): owner_first = owners[first_block]  38.4 us
  transfers between devices with their start and end apart: 4, of which 0 were waited for; matrix products, arithmetic and copies ran while one was open for 97% of the time, Pallas kernels for 0%

commit v1 on v0

v1 whole, which is shorter than its diff:
```python
import functools

import jax
import jax.numpy as jnp
from jax import lax
from jax.experimental import pallas as pl
from jax.experimental.pallas import tpu as pltpu
from jax.sharding import PartitionSpec as P

CHUNKS = (1536, 512)
MIB = 1024 * 1024
MAIN_LIMIT, EARLY_LIMIT, LATE_LIMIT = 20 * MIB, 12 * MIB, 12 * MIB
F32 = jnp.float32


def dot_rows(left, right):
    return lax.dot_general(left, right, (((1,), (1,)), ((), ())), preferred_element_type=F32)


def flat(block):
    return block.reshape(block.shape[0] * block.shape[1], block.shape[2])


def layout(cap, me, slots_ref):
    even = me % 2 == 0
    start = me // 2 * 4
    odd_live = slots_ref[start + 3] % cap + 1
    live = jnp.where(even, 4 - odd_live, odd_live)
    return live, jnp.where(even, start, start + 4 - odd_live), even


def in_hbm(value):
    return pltpu.with_memory_space_constraint(value, pltpu.HBM)


def pick_kernel(cap, spans, me_ref, slots_ref, own_ref, *refs):
    outs, sems = refs[:-1], refs[-1]
    live, _, even = layout(cap, me_ref[0], slots_ref)
    slot = jnp.where(even, 0, live - 1)
    copies = []
    for n, (start, size) in enumerate(spans):
        for k in range(3):
            copies.append(
                pltpu.make_async_copy(
                    own_ref.at[slot, k, :, pl.ds(start, size)], outs[n].at[k], sems.at[n, k]
                )
            )
    for copy in copies:
        copy.start()
    for copy in copies:
        copy.wait()


def pick(me, block_slot, own, spans):
    cap, aux, rows, _ = own.shape
    hbm = pl.BlockSpec(memory_space=pltpu.HBM)
    moved = sum(size for _, size in spans) * aux * rows * 4
    return pl.pallas_call(
        functools.partial(pick_kernel, cap, spans),
        out_shape=tuple(jax.ShapeDtypeStruct((aux, rows, size), own.dtype) for _, size in spans),
        in_specs=[
            pl.BlockSpec(memory_space=pltpu.SMEM),
            pl.BlockSpec(memory_space=pltpu.SMEM),
            hbm,
        ],
        out_specs=(pl.BlockSpec(memory_space=pltpu.VMEM),) * len(spans),
        scratch_shapes=[pltpu.SemaphoreType.DMA((len(spans), aux))],
        name="pick",
        cost_estimate=pl.CostEstimate(flops=0, bytes_accessed=moved, transcendentals=0),
    )(me.reshape(1), block_slot, in_hbm(own))


def counts_kernel(cap, me_ref, slots_ref, pairs_ref, domain_ref, counts_ref, meta_ref):
    live, first, even = layout(cap, me_ref[0], slots_ref)
    meta_ref[0] = live
    meta_ref[1] = even.astype(jnp.int32)
    meta_ref[2] = jnp.where(even, 0, live - 1)
    meta_ref[3] = jnp.where(live == 1, 0, jnp.where(even, 1, live - 2))
    meta_ref[4] = jnp.where(even, live - 1, 0)
    meta_ref[5] = jnp.where(live == 1, 0, jnp.where(even, live - 2, 1))
    meta_ref[6] = jnp.where(even, 0, cap - live)
    meta_ref[7] = 0
    a = pairs_ref[0:1, :]
    b = pairs_ref[1:2, :]
    edge = (a - (first - 1)) * 2 + (b - a - 1)
    size = a.shape[1]
    rows = lax.broadcasted_iota(jnp.int32, (16, size), 0)
    hot = jnp.where(rows == edge, 1.0, 0.0).astype(jnp.bfloat16)
    weight = jnp.zeros((16, size), F32)
    for j in range(2):
        code = domain_ref[j : j + 1, :] * 3 + domain_ref[j + 2 : j + 3, :]
        weight = weight + jnp.where(rows == code, 1.0, 0.0)
    counts_ref[...] = dot_rows(hot, weight.astype(jnp.bfloat16))


def pair_counts(me, block_slot, pair_list, domain_slots, cap):
    pairs, domain = pair_list.T, domain_slots.T
    vmem = pl.BlockSpec(memory_space=pltpu.VMEM)
    smem = pl.BlockSpec(memory_space=pltpu.SMEM)
    return pl.pallas_call(
        functools.partial(counts_kernel, cap),
        out_shape=(jax.ShapeDtypeStruct((16, 16), F32), jax.ShapeDtypeStruct((8,), jnp.int32)),
        in_specs=[smem, smem, vmem, vmem],
        out_specs=(vmem, smem),
        name="pair_counts",
        cost_estimate=pl.CostEstimate(flops=4_000_000, bytes_accessed=200_000, transcendentals=0),
    )(me.reshape(1), block_slot, pairs, domain)


def weigh(counts_ref, row, step_left, step_right, left, right_of, total_ref):
    rows = left.shape[0] // 3

    for l in range(3):
        product = dot_rows(left, right_of(l))
        total = total_ref[...]
        for k in range(3):
            count = counts_ref[row, k * step_left + l * step_right]
            total = total + count * product[k * rows : (k + 1) * rows]
        total_ref[...] = total


def split(counts_ref, row, step_own, step_halo, aux_of, l):
    total = None
    for k in range(3):
        part = counts_ref[row, k * step_own + l * step_halo] * aux_of(k).astype(F32)
        total = part if total is None else total + part
    high = total.astype(jnp.bfloat16)
    return high, (total - high.astype(F32)).astype(jnp.bfloat16)


def main_kernel(
    meta_ref, counts_ref, own_hbm, partner_hbm, sum_ref, back_ref, mix_early, mix_late, own_ref, inner_ref, edge_ref, sems
):
    live, even = meta_ref[0], meta_ref[1] == 1
    adj_out, sec_out, adjacent, second = meta_ref[2], meta_ref[3], meta_ref[4], meta_ref[5]
    adj_mine = (live == 1) | ((live == 2) & even)
    step_own = jnp.where(even, 3, 1)
    step_halo = jnp.where(even, 1, 3)
    rows = own_ref.shape[2]

    def own_copy(s):
        return pltpu.make_async_copy(own_hbm.at[s], own_ref.at[s], sems.at[s])

    inner_copy = pltpu.make_async_copy(partner_hbm.at[meta_ref[6]], inner_ref, sems.at[3])
    for s in range(3):
        own_copy(s).start()
    inner_copy.start()
    back_ref[...] = jnp.zeros_like(back_ref)
    def diag(s, carry):
        own_copy(s).wait()

        @pl.when(s < live)
        def _():
            total = dot_rows(own_ref[s, 0], own_ref[s, 0])
            for k in range(1, 3):
                total = total + dot_rows(own_ref[s, k], own_ref[s, k])
            sum_ref[s] = total

        @pl.when(s >= live)
        def _():
            sum_ref[s] = jnp.zeros((rows, rows), F32)

        return carry

    lax.fori_loop(0, 3, diag, 0)

    def own_edge(e, carry):
        i, j = e // 2, jnp.minimum(e + 1, 2)

        @pl.when(j < live)
        def _():
            row = (i + 1) * 2 + (j - i - 1)
            edge_ref[...] = jnp.zeros_like(edge_ref)
            weigh(counts_ref, row, 3, 1, flat(own_ref[i]), lambda l: own_ref[j, l], edge_ref)
            sum_ref[i] += edge_ref[...]
            sum_ref[j] += edge_ref[...].T

        return carry

    lax.fori_loop(0, 3, own_edge, 0)

    inner_copy.wait()

    def put(e, row, source):
        def one(n, carry):
            l, r = n // (rows // 32), pl.multiple_of(n % (rows // 32) * 32, 32)
            high, low = split(counts_ref, row, step_halo, step_own, lambda k: source(k, r), l)
            early = mix_early.shape[-1]
            for part, values in ((0, high), (1, low)):
                where = pl.ds((2 * e + part) * rows + r, 32)
                mix_early[l, where] = values[:, :early]
                mix_late[l, where] = values[:, early:]
            return carry

        lax.fori_loop(0, 3 * rows // 32, one, 0)

    row_adj = jnp.where(even, 0, live * 2)
    row_sec = jnp.where(even, 1, (live - 1) * 2 + 1)
    put(0, row_adj, lambda k, r: own_ref[adj_out, k, pl.ds(r, 32)])

    @pl.when(live >= 2)
    def _():
        put(1, row_sec, lambda k, r: own_ref[sec_out, k, pl.ds(r, 32)])

    @pl.when(live == 1)
    def _():
        put(1, row_sec, lambda k, r: inner_ref[k, pl.ds(r, 32)])

    def inner_edge(e, carry):
        slot = jnp.where(e == 0, adjacent, second)

        @pl.when(jnp.where(e == 0, adj_mine, live >= 2))
        def _():
            row = jnp.where(even, jnp.where(e == 0, live * 2, (live - 1) * 2 + 1), e)
            edge_ref[...] = jnp.zeros_like(edge_ref)
            weigh(
                counts_ref, row, step_own, step_halo, flat(own_ref[slot]), lambda l: inner_ref[l], edge_ref
            )
            sum_ref[slot] += edge_ref[...]
            back_ref[...] += edge_ref[...].T

        return carry

    lax.fori_loop(0, 2, inner_edge, 0)


def main_part(meta, counts, own, partner):
    cap, aux, rows, width = own.shape
    smem = pl.BlockSpec(memory_space=pltpu.SMEM)
    vmem = pl.BlockSpec(memory_space=pltpu.VMEM)
    hbm = pl.BlockSpec(memory_space=pltpu.HBM)
    return pl.pallas_call(
        main_kernel,
        in_specs=[smem, smem, hbm, pl.BlockSpec(memory_space=pl.ANY)],
        out_specs=(vmem, vmem, vmem, vmem),
        scratch_shapes=[
            pltpu.VMEM((cap, aux, rows, width), own.dtype),
            pltpu.VMEM((aux, rows, width), own.dtype),
            pltpu.VMEM((rows, rows), F32),
            pltpu.SemaphoreType.DMA((4,)),
        ],
        out_shape=(
            jax.ShapeDtypeStruct((cap, rows, rows), F32),
            jax.ShapeDtypeStruct((rows, rows), F32),
            pltpu.VMEM((aux, 4 * rows, CHUNKS[0]), own.dtype),
            pltpu.VMEM((aux, 4 * rows, CHUNKS[1]), own.dtype),
        ),
        compiler_params=pltpu.CompilerParams(vmem_limit_bytes=MAIN_LIMIT),
        name="own_and_inner",
        cost_estimate=pl.CostEstimate(
            flops=60 * 2 * rows * rows * width, bytes_accessed=26_000_000, transcendentals=0
        ),
    )(meta, counts, in_hbm(own), partner)


def mixed(mix_ref, outer_ref):
    total = None
    for l in range(3):
        part = dot_rows(mix_ref[l], outer_ref[l])
        total = part if total is None else total + part
    rows = total.shape[0] // 4
    return total[:rows] + total[rows : 2 * rows], total[2 * rows : 3 * rows] + total[3 * rows :]


def early_kernel(mix_ref, outer_ref, adj_ref, sec_ref):
    adj_ref[...], sec_ref[...] = mixed(mix_ref, outer_ref)


def early_part(mix, outer):
    aux, rows, width = outer.shape
    vmem = pl.BlockSpec(memory_space=pltpu.VMEM)
    return pl.pallas_call(
        early_kernel,
        in_specs=[vmem] * 2,
        out_specs=(vmem,) * 2,
        out_shape=(jax.ShapeDtypeStruct((rows, rows), F32),) * 2,
        compiler_params=pltpu.CompilerParams(vmem_limit_bytes=EARLY_LIMIT),
        name="outer_early",
        cost_estimate=pl.CostEstimate(
            flops=12 * 2 * rows * rows * width, bytes_accessed=1_000_000, transcendentals=0
        ),
    )(mix, outer)


def late_kernel(meta_ref, mix_ref, outer_ref, adj_in, sec_in, inner_in, back_ref, inner_ref, adj_ref, sec_ref):
    adj, sec = mixed(mix_ref, outer_ref)
    sec = sec_in[...] + sec
    back_ref[...] = sec.T
    sec_ref[...] = sec
    inner_ref[...] = inner_in[...] + jnp.where(meta_ref[0] == 1, sec, 0.0)
    adj_ref[...] = adj_in[...] + adj


def late_part(meta, mix, outer, adj, sec, inner_back):
    aux, rows, width = outer.shape
    square = jax.ShapeDtypeStruct((rows, rows), F32)
    vmem = pl.BlockSpec(memory_space=pltpu.VMEM)
    return pl.pallas_call(
        late_kernel,
        in_specs=[pl.BlockSpec(memory_space=pltpu.SMEM)] + [vmem] * 5,
        out_specs=(vmem,) * 4,
        out_shape=(square,) * 4,
        compiler_params=pltpu.CompilerParams(vmem_limit_bytes=LATE_LIMIT),
        name="outer_late",
        cost_estimate=pl.CostEstimate(
            flops=12 * 2 * rows * rows * width, bytes_accessed=6_000_000, transcendentals=0
        ),
    )(meta, mix, outer, adj, sec, inner_back)


def settle_kernel(meta_ref, sum_ref, adj_ref, sec_ref, out_ref):
    out_ref[...] = sum_ref[...]
    out_ref[meta_ref[2]] += adj_ref[...]

    @pl.when(meta_ref[0] >= 2)
    def _():
        out_ref[meta_ref[3]] += sec_ref[...]


def finish_kernel(meta_ref, sum_ref, outer_ref, inner_ref, out_ref):
    out_ref[...] = sum_ref[...]
    out_ref[meta_ref[2]] += outer_ref[...]
    out_ref[meta_ref[4]] += inner_ref[...]


def add_blocks(kernel, name, meta, total, first, second):
    vmem = pl.BlockSpec(memory_space=pltpu.VMEM)
    return pl.pallas_call(
        kernel,
        in_specs=[pl.BlockSpec(memory_space=pltpu.SMEM)] + [vmem] * 3,
        out_specs=vmem,
        out_shape=jax.ShapeDtypeStruct(total.shape, F32),
        compiler_params=pltpu.CompilerParams(vmem_limit_bytes=LATE_LIMIT),
        name=name,
        cost_estimate=pl.CostEstimate(flops=200_000, bytes_accessed=2_000_000, transcendentals=0),
    )(meta, total, first, second)


def per_device(own, block_slot, pair_list, domain_slots):
    cap = own.shape[0]
    count = lax.axis_size("blk")
    me = lax.axis_index("blk")
    to_outer = [(d, d - 1) for d in range(2, count, 2)] + [(d, d + 1) for d in range(1, count - 1, 2)]
    to_inner = [(d, d ^ 1) for d in range(count)]
    first, late = CHUNKS
    (early_piece,) = pick(me, block_slot, own, [(0, first)])
    outer_early = lax.ppermute(early_piece, "blk", to_outer)
    (late_piece,) = pick(me, block_slot, own, [(first, late)])
    outer_late = lax.ppermute(late_piece, "blk", to_outer)
    partner = lax.ppermute(own, "blk", to_inner)
    counts, meta = pair_counts(me, block_slot, pair_list, domain_slots, cap)
    own_sum, inner_back, mix_early, mix_late = main_part(meta, counts, own, partner)
    adj, sec = early_part(mix_early, outer_early)
    outer_back, inner_back, adj, sec = late_part(meta, mix_late, outer_late, adj, sec, inner_back)
    from_outer = lax.ppermute(outer_back, "blk", to_outer)
    from_inner = lax.ppermute(inner_back, "blk", to_inner)
    total = add_blocks(settle_kernel, "settle", meta, own_sum, adj, sec)
    return add_blocks(finish_kernel, "finish", meta, total, from_outer, from_inner)


def solution(mesh):
    placed = (P("blk", None, None, None), P(), P(), P())
    return jax.shard_map(
        per_device, mesh=mesh, in_specs=placed, out_specs=P("blk", None, None), check_vma=False
    )
```

time: 520 us -> 62.8 us (0.12); the launches traced: 512 us -> 62.5 us
  matrix products: 327 us -> 0 us
  local copies, waits for them, and re-layouts: 165 us -> 1.31 us
  Pallas kernels: 0 us -> 36.6 us
  waiting for transfers between devices: 0.01 us -> 10.9 us
    dot_general x15 -> x0, matrix products: 327 us -> none  [the longest x3 81.2 us: per_device(): jnp.einsum('blyx,blix->byi', source.astype(jnp.float32), right_sum, preci...]
    gather x4 -> x0, local copies, waits for them, and re-layouts: 153 us -> none  [the longest x1 38.4 us: per_device(): slot_second = local_slot[second_block]]
    pallas_call x0 -> x8, Pallas kernels: none -> 36.6 us  [the longest x1 21.9 us: main_part(): pl.pallas_call(main_kernel, in_specs=[smem, smem, hbm, pl.BlockSpec(memor...]
    ppermute x4 -> x5, waiting for transfers between devices: 0.01 us -> 10.9 us  [the longest x1 8.14 us: per_device(): from_outer = lax.ppermute(outer_back, 'blk', to_outer)]
    dot_general x1 -> x0, local copies, waits for them, and re-layouts: 7.92 us -> none  [per_device(): aux_pairs = jnp.einsum('pjk,pjl->pkl', left_aux, right_aux)]
    ppermute x4 -> x5, starting transfers between devices: 15.1 us -> 13.5 us  [the longest x1 6.77 us: per_device(): outer_late = lax.ppermute(late_piece, 'blk', to_outer)]
  transfers between devices with their start and end apart: 4 -> 5, of which waited for: 0 -> 2; matrix products, arithmetic and copies ran while one was open for 97% -> 0% of each run, Pallas kernels for 0% -> 53%
where the time goes in v1:
time: 62.8 us; the launch traced here: 62.5 us
  Pallas kernels  36.6 us (58%)
  starting transfers between devices  13.5 us (21%)
  waiting for transfers between devices  10.9 us (17%)
  local copies, waits for them, and re-layouts  1.31 us (2%)
    pallas_call x1, Pallas kernels, main_part(): pl.pallas_call(main_kernel, in_specs=[smem, smem, hbm, pl.BlockSpec(memor...  21.9 us
    ppermute x1, waiting for transfers between devices, per_device(): from_outer = lax.ppermute(outer_back, 'blk', to_outer)  8.14 us
    ppermute x1, starting transfers between devices, per_device(): outer_late = lax.ppermute(late_piece, 'blk', to_outer)  6.77 us
    pallas_call x2, Pallas kernels, pick(): pl.pallas_call(functools.partial(pick_kernel, cap, spans), out_shape=tupl...  6.46 us
    ppermute x1, starting transfers between devices, per_device(): from_outer = lax.ppermute(outer_back, 'blk', to_outer)  3.01 us
    ppermute x1, starting transfers between devices, per_device(): outer_early = lax.ppermute(early_piece, 'blk', to_outer)  3.01 us
    ppermute x1, waiting for transfers between devices, per_device(): outer_late = lax.ppermute(late_piece, 'blk', to_outer)  2.79 us
    pallas_call x1, Pallas kernels, early_part(): pl.pallas_call(early_kernel, in_specs=[vmem] * 2, out_specs=(vmem,) * 2,...  2.62 us
  transfers between devices with their start and end apart: 5, of which 2 were waited for; matrix products, arithmetic and copies ran while one was open for 0% of the time, Pallas kernels for 53%

profile of v1, /device:TPU:63, one launch (start us, length us, event | category | flops | bytes accessed | tf_op | source)
XLA Modules:
  0.0 62.5 jit_solution(4023989898030743027)
XLA Ops:
  0.0 0.7 %collective-permute-start = (bf16[3,3,256,2048]{3,2,1,0:T(8,128)(2,1)}, bf16[3,3,256,2048]{3,2,1,0:T(8,128)(2,1)}, u32[]{:S(2)}, u32[]{:S(2)}) collective-permute-start(bf16[3,3,256,2048]{3,2,1,0:T(8,128)(2,1)} %own_ref.3), channel_id=1, source_target_pairs={{0,1},{1,0},{2,3},{3,2},{4,5},{5,4},{6,7},{7,6},{8,9},{9,8},{10,11... | collective-permute-start | bytes 28311560 | tf_op jit(solution)/shard_map/ppermute | solution.py:350
  0.7 3.7 %pick.3 = bf16[3,256,1536]{2,1,0:T(8,128)(2,1)} custom-call(s32[1]{0:T(128)} %bitcast.me_ref, s32[256]{0:T(256)} %slots_ref.5, bf16[3,3,256,2048]{3,2,1,0:T(8,128)(2,1)} %own_ref.3), custom_call_target="tpu_custom_call" | custom-call | bytes 4718592 | tf_op jit(solution)/shard_map/pick/pallas_call | solution.py:58
  4.4 3.0 %collective-permute-start.2 = (bf16[3,256,1536]{2,1,0:T(8,128)(2,1)}, bf16[3,256,1536]{2,1,0:T(8,128)(2,1)S(1)}, u32[]{:S(2)}, u32[]{:S(2)}) collective-permute-start(bf16[3,256,1536]{2,1,0:T(8,128)(2,1)} %pick.3), channel_id=1, source_target_pairs={{2,1},{4,3},{6,5},{8,7},{10,9},{12,11},{14,13},{16,15},{18,17},{20... | collective-permute-start | bytes 7077896 | tf_op jit(solution)/shard_map/ppermute | solution.py:347
  7.4 2.7 %pick.2 = bf16[3,256,512]{2,1,0:T(8,128)(2,1)} custom-call(s32[1]{0:T(128)} %bitcast.me_ref, s32[256]{0:T(256)} %slots_ref.5, bf16[3,3,256,2048]{3,2,1,0:T(8,128)(2,1)} %own_ref.3), custom_call_target="tpu_custom_call" | custom-call | bytes 1572864 | tf_op jit(solution)/shard_map/pick/pallas_call | solution.py:58
  10.2 6.8 %collective-permute-start.1 = (bf16[3,256,512]{2,1,0:T(8,128)(2,1)}, bf16[3,256,512]{2,1,0:T(8,128)(2,1)S(1)}, u32[]{:S(2)}, u32[]{:S(2)}) collective-permute-start(bf16[3,256,512]{2,1,0:T(8,128)(2,1)} %pick.2), channel_id=1, source_target_pairs={{2,1},{4,3},{6,5},{8,7},{10,9},{12,11},{14,13},{16,15},{18,17},{20... | collective-permute-start | bytes 2359304 | tf_op jit(solution)/shard_map/ppermute | solution.py:349
  16.9 1.8 %pair_counts.1 = (f32[16,16]{1,0:T(8,128)}, s32[8]{0:T(128)}) custom-call(s32[1]{0:T(128)} %bitcast.me_ref, s32[256]{0:T(256)} %slots_ref.5, s32[2,6144]{1,0:T(2,128)} %bitcast.4, s32[4,6144]{1,0:T(4,128)} %bitcast.3), custom_call_target="tpu_custom_call" | custom-call | flops 4000000 | bytes 200000 | tf_op jit(solution)/shard_map/pair_counts/pallas_call | solution.py:100
  18.7 0.0 collective-permute-done.partner_hbm
  18.7 0.0 copy-start
  18.8 0.6 copy-done
  19.4 0.0 copy-start.1
  19.4 0.7 %copy-done.1 = f32[16,16]{1,0:T(8,128)S(1)} copy-done((f32[16,16]{1,0:T(8,128)S(1)}, f32[16,16]{1,0:T(8,128)}, u32[]{:S(2)}) %copy-start.1) | copy-done | bytes 1048
  20.1 21.9 %own_and_inner.1 = (f32[3,256,256]{2,1,0:T(8,128)S(1)}, f32[256,256]{1,0:T(8,128)S(1)}, bf16[3,1024,1536]{2,1,0:T(8,128)(2,1)S(1)}, bf16[3,1024,512]{2,1,0:T(8,128)(2,1)S(1)}) custom-call(s32[8]{0:T(128)S(1)} %copy-done, f32[16,16]{1,0:T(8,128)S(1)} %copy-done.1, bf16[3,3,256,2048]{3,2,1,0:T(8,128)(2,1)} %own_ref.3, ...), custom_call_target="tpu_custom_call" | custom-call | flops 16106127360 | bytes 26000000 | tf_op jit(solution)/shard_map/own_and_inner/pallas_call | solution.py:232
  42.0 0.0 collective-permute-done.2.outer_ref
  42.0 2.6 %outer_early.1 = (f32[256,256]{1,0:T(8,128)S(1)}, f32[256,256]{1,0:T(8,128)S(1)}) custom-call(bf16[3,1024,1536]{2,1,0:T(8,128)(2,1)S(1)} %get-tuple-element.21.mix_ref, bf16[3,256,1536]{2,1,0:T(8,128)(2,1)S(1)} %collective-permute-done.2.outer_ref), custom_call_target="tpu_custom_call" | custom-call | flops 2415919104 | bytes 1000000 | tf_op jit(solution)/shard_map/outer_early/pallas_call | solution.py:272
  44.6 2.8 %collective-permute-done.1.outer_ref = bf16[3,256,512]{2,1,0:T(8,128)(2,1)S(1)} collective-permute-done((bf16[3,256,512]{2,1,0:T(8,128)(2,1)}, bf16[3,256,512]{2,1,0:T(8,128)(2,1)S(1)}, u32[]{:S(2)}, u32[]{:S(2)}) %collective-permute-start.1) | collective-permute-done | bytes 786464 | tf_op jit(solution)/shard_map/ppermute | solution.py:349
  47.4 1.6 %outer_late.1 = (f32[256,256]{1,0:T(8,128)S(1)}, f32[256,256]{1,0:T(8,128)S(1)}, f32[256,256]{1,0:T(8,128)S(1)}, f32[256,256]{1,0:T(8,128)S(1)}) custom-call(s32[8]{0:T(128)S(1)} %copy-done, bf16[3,1024,512]{2,1,0:T(8,128)(2,1)S(1)} %get-tuple-element.20.mix_ref, bf16[3,256,512]{2,1,0:T(8,128)(2,1)S(1)} %collective-permute-done.1.outer_ref, ...), custom_call_target="tpu_custom_call" | custom-call | flops 805306368 | bytes 6000000 | tf_op jit(solution)/shard_map/outer_late/pallas_call | solution.py:298
  49.1 3.0 %collective-permute-start.3 = (f32[256,256]{1,0:T(8,128)S(1)}, f32[256,256]{1,0:T(8,128)S(1)}, u32[]{:S(2)}, u32[]{:S(2)}) collective-permute-start(f32[256,256]{1,0:T(8,128)S(1)} %get-tuple-element.27), channel_id=1, source_target_pairs={{2,1},{4,3},{6,5},{8,7},{10,9},{12,11},{14,13},{16,15},{18,17},{20... | collective-permute-start | bytes 786440 | tf_op jit(solution)/shard_map/ppermute | solution.py:355
  52.1 0.1 collective-permute-start.4
  52.2 0.6 %settle.1.sum_ref = f32[3,256,256]{2,1,0:T(8,128)S(1)} custom-call(s32[8]{0:T(128)S(1)} %copy-done, f32[3,256,256]{2,1,0:T(8,128)S(1)} %get-tuple-element.19.sum_ref, f32[256,256]{1,0:T(8,128)S(1)} %get-tuple-element.25.adj_ref, f32[256,256]{1,0:T(8,128)S(1)} %get-tuple-element.26.sec_ref), custom_call_target="tpu_custom_call" | custom-call | flops 200000 | bytes 2000000 | tf_op jit(solution)/shard_map/settle/pallas_call | solution.py:328
  52.8 8.1 %collective-permute-done.3.outer_ref = f32[256,256]{1,0:T(8,128)S(1)} collective-permute-done((f32[256,256]{1,0:T(8,128)S(1)}, f32[256,256]{1,0:T(8,128)S(1)}, u32[]{:S(2)}, u32[]{:S(2)}) %collective-permute-start.3) | collective-permute-done | bytes 262176 | tf_op jit(solution)/shard_map/ppermute | solution.py:355
  61.0 0.0 collective-permute-done.4.inner_ref
  61.0 1.5 %finish.1 = f32[3,256,256]{2,1,0:T(8,128)} custom-call(s32[8]{0:T(128)S(1)} %copy-done, f32[3,256,256]{2,1,0:T(8,128)S(1)} %settle.1.sum_ref, f32[256,256]{1,0:T(8,128)S(1)} %collective-permute-done.3.outer_ref, f32[256,256]{1,0:T(8,128)S(1)} %collective-permute-done.4.inner_ref), custom_call_target="tpu_custom_call" | custom-call | flops 200000 | bytes 2000000 | tf_op jit(solution)/shard_map/finish/pallas_call | solution.py:328
Async XLA Ops:
  0.0 18.7 %collective-permute-start = (bf16[3,3,256,2048]{3,2,1,0:T(8,128)(2,1)}, bf16[3,3,256,2048]{3,2,1,0:T(8,128)(2,1)}, u32[]{:S(2)}, u32[]{:S(2)}) collective-permute-start(bf16[3,3,256,2048]{3,2,1,0:T(8,128)(2,1)} %own_ref.3), channel_id=1, source_target_pairs={{0,1},{1,0},{2,3},{3,2},{4,5},{5,4},{6,7},{7,6},{8,9},{9,8},{10,11... | collective-permute-start | bytes 28311560 | tf_op jit(solution)/shard_map/ppermute | solution.py:350
  4.4 37.6 %collective-permute-start.2 = (bf16[3,256,1536]{2,1,0:T(8,128)(2,1)}, bf16[3,256,1536]{2,1,0:T(8,128)(2,1)S(1)}, u32[]{:S(2)}, u32[]{:S(2)}) collective-permute-start(bf16[3,256,1536]{2,1,0:T(8,128)(2,1)} %pick.3), channel_id=1, source_target_pairs={{2,1},{4,3},{6,5},{8,7},{10,9},{12,11},{14,13},{16,15},{18,17},{20... | collective-permute-start | bytes 7077896 | tf_op jit(solution)/shard_map/ppermute | solution.py:347
  10.2 37.3 %collective-permute-start.1 = (bf16[3,256,512]{2,1,0:T(8,128)(2,1)}, bf16[3,256,512]{2,1,0:T(8,128)(2,1)S(1)}, u32[]{:S(2)}, u32[]{:S(2)}) collective-permute-start(bf16[3,256,512]{2,1,0:T(8,128)(2,1)} %pick.2), channel_id=1, source_target_pairs={{2,1},{4,3},{6,5},{8,7},{10,9},{12,11},{14,13},{16,15},{18,17},{20... | collective-permute-start | bytes 2359304 | tf_op jit(solution)/shard_map/ppermute | solution.py:349
  18.7 0.6 %copy-start = (s32[8]{0:T(128)S(1)}, s32[8]{0:T(128)}, u32[]{:S(2)}) copy-start(s32[8]{0:T(128)} %get-tuple-element.17.meta_ref) | copy-start | bytes 100
  19.4 0.7 %copy-start.1 = (f32[16,16]{1,0:T(8,128)S(1)}, f32[16,16]{1,0:T(8,128)}, u32[]{:S(2)}) copy-start(f32[16,16]{1,0:T(8,128)} %get-tuple-element.18.counts_ref) | copy-start | bytes 3076
  49.1 11.9 %collective-permute-start.3 = (f32[256,256]{1,0:T(8,128)S(1)}, f32[256,256]{1,0:T(8,128)S(1)}, u32[]{:S(2)}, u32[]{:S(2)}) collective-permute-start(f32[256,256]{1,0:T(8,128)S(1)} %get-tuple-element.27), channel_id=1, source_target_pairs={{2,1},{4,3},{6,5},{8,7},{10,9},{12,11},{14,13},{16,15},{18,17},{20... | collective-permute-start | bytes 786440 | tf_op jit(solution)/shard_map/ppermute | solution.py:355
  52.1 8.9 %collective-permute-start.4 = (f32[256,256]{1,0:T(8,128)S(1)}, f32[256,256]{1,0:T(8,128)S(1)}, u32[]{:S(2)}, u32[]{:S(2)}) collective-permute-start(f32[256,256]{1,0:T(8,128)S(1)} %get-tuple-element.28), channel_id=1, source_target_pairs={{0,1},{1,0},{2,3},{3,2},{4,5},{5,4},{6,7},{7,6},{8,9},{9,8},{10,11... | collective-permute-start | bytes 786440 | tf_op jit(solution)/shard_map/ppermute | solution.py:356

commit v2 on v1

v2 whole, which is shorter than its diff:
```python
import functools

import jax
import jax.numpy as jnp
from jax import lax
from jax.experimental import pallas as pl
from jax.experimental.pallas import tpu as pltpu
from jax.sharding import PartitionSpec as P

EARLY = 1792
MIB = 1024 * 1024
MAIN_LIMIT, EARLY_LIMIT, LATE_LIMIT = 24 * MIB, 12 * MIB, 12 * MIB
F32 = jnp.float32
BLOCK = 256
TOKEN = pltpu.VMEM((8, 128), jnp.float32)


def dot_rows(left, right):
    return lax.dot_general(left, right, (((1,), (1,)), ((), ())), preferred_element_type=F32)


def flat(block):
    return block.reshape(block.shape[0] * block.shape[1], block.shape[2])


def layout(cap, me, slots_ref):
    even = me % 2 == 0
    start = me // 2 * 4
    odd_live = slots_ref[start + 3] % cap + 1
    live = jnp.where(even, 4 - odd_live, odd_live)
    return live, jnp.where(even, start, start + 4 - odd_live), even


def in_hbm(value):
    return pltpu.with_memory_space_constraint(value, pltpu.HBM)


def run_copies(pairs, sems):
    copies = [pltpu.make_async_copy(source, target, sems.at[n]) for n, (source, target) in enumerate(pairs)]
    for copy in copies:
        copy.start()
    for copy in copies:
        copy.wait()


def pick_kernel(cap, me_ref, slots_ref, own_ref, out_ref, sems):
    live, _, even = layout(cap, me_ref[0], slots_ref)
    slot = jnp.where(even, 0, live - 1)
    width = out_ref.shape[-1]
    part = own_ref.shape[2] // 4
    run_copies(
        [
            (
                own_ref.at[slot, k, pl.ds(q * part, part), pl.ds(0, width)],
                out_ref.at[k, pl.ds(q * part, part)],
            )
            for k in range(3)
            for q in range(4)
        ],
        sems,
    )


def pick_two_kernel(cap, start, me_ref, slots_ref, own_ref, partner_ref, after, out_ref, token_ref, sems):
    del after
    token_ref[...] = jnp.zeros_like(token_ref)
    live, _, even = layout(cap, me_ref[0], slots_ref)
    width = out_ref.shape[-1]
    columns = pl.ds(start, width)
    slot = jnp.where(even, 0, live - 1)
    first = [(own_ref.at[slot, k, :, columns], out_ref.at[0, k]) for k in range(3)]

    @pl.when(live >= 2)
    def _():
        second = jnp.where(even, 1, live - 2)
        run_copies(first + [(own_ref.at[second, k, :, columns], out_ref.at[1, k]) for k in range(3)], sems)

    @pl.when(live == 1)
    def _():
        second = jnp.where(even, 0, cap - live)
        run_copies(first + [(partner_ref.at[second, k, :, columns], out_ref.at[1, k]) for k in range(3)], sems)


def pick_call(kernel, name, shape, me, block_slot, blocks, *after):
    smem = pl.BlockSpec(memory_space=pltpu.SMEM)
    moved = 4
    for size in shape:
        moved *= size
    return pl.pallas_call(
        kernel,
        out_shape=(pltpu.VMEM(shape, blocks[0].dtype),) + (TOKEN,) * (len(blocks) - 1),
        in_specs=[smem, smem, pl.BlockSpec(memory_space=pltpu.HBM)]
        + [pl.BlockSpec(memory_space=pl.ANY)] * (len(blocks) - 1 + len(after)),
        out_specs=(pl.BlockSpec(memory_space=pltpu.VMEM),) * len(blocks),
        scratch_shapes=[pltpu.SemaphoreType.DMA((12,))],
        compiler_params=pltpu.CompilerParams(vmem_limit_bytes=LATE_LIMIT),
        name=name,
        cost_estimate=pl.CostEstimate(flops=0, bytes_accessed=moved, transcendentals=0),
    )(me.reshape(1), in_hbm(block_slot), in_hbm(blocks[0]), *blocks[1:], *after)


def pick_early(me, block_slot, own):
    cap, aux, rows, _ = own.shape
    return pick_call(
        functools.partial(pick_kernel, cap), "pick", (aux, rows, EARLY), me, block_slot, [own]
    )[0]


def pick_late(me, block_slot, own, partner, after):
    cap, aux, rows, width = own.shape
    return pick_call(
        functools.partial(pick_two_kernel, cap, EARLY),
        "pick_two",
        (2, aux, rows, width - EARLY),
        me,
        block_slot,
        [own, partner],
        after,
    )


def counts_kernel(cap, me_ref, slots_ref, pairs_ref, domain_ref, counts_ref, meta_ref):
    live, first, even = layout(cap, me_ref[0], slots_ref)
    values = (
        live,
        even.astype(jnp.int32),
        jnp.where(even, 0, live - 1),
        jnp.where(live == 1, 0, jnp.where(even, 1, live - 2)),
        jnp.where(even, live - 1, 0),
        jnp.where(live == 1, 0, jnp.where(even, live - 2, 1)),
        jnp.where(even, 0, cap - live),
    )
    lanes = lax.broadcasted_iota(jnp.int32, meta_ref.shape, 1)
    meta = jnp.zeros(meta_ref.shape, jnp.int32)
    for n, value in enumerate(values):
        meta = jnp.where(lanes == n, value, meta)
    meta_ref[...] = meta
    a = pairs_ref[0:1, :]
    b = pairs_ref[1:2, :]
    edge = (a - (first - 2)) * 2 + (b - a - 1)
    size = a.shape[1]
    rows = lax.broadcasted_iota(jnp.int32, (16, size), 0)
    hot = jnp.where(rows == edge, 1.0, 0.0).astype(jnp.bfloat16)
    weight = jnp.zeros((16, size), F32)
    for j in range(2):
        code = domain_ref[j : j + 1, :] * 3 + domain_ref[j + 2 : j + 3, :]
        weight = weight + jnp.where(rows == code, 1.0, 0.0)
    counts_ref[...] = dot_rows(hot, weight.astype(jnp.bfloat16))


def pair_counts(me, block_slot, pair_list, domain_slots, cap):
    pairs, domain = pair_list.T, domain_slots.T
    vmem = pl.BlockSpec(memory_space=pltpu.VMEM)
    smem = pl.BlockSpec(memory_space=pltpu.SMEM)
    return pl.pallas_call(
        functools.partial(counts_kernel, cap),
        out_shape=(pltpu.VMEM((16, 16), F32), pltpu.VMEM((8, 128), jnp.int32)),
        in_specs=[smem, smem, vmem, vmem],
        out_specs=(vmem, vmem),
        compiler_params=pltpu.CompilerParams(vmem_limit_bytes=LATE_LIMIT),
        name="pair_counts",
        cost_estimate=pl.CostEstimate(flops=4_000_000, bytes_accessed=200_000, transcendentals=0),
    )(me.reshape(1), block_slot, pairs, domain)


def weigh(counts_ref, row, step_left, step_right, left, right_of, total_ref):
    rows = left.shape[0] // 3

    for l in range(3):
        product = dot_rows(left, right_of(l))
        total = total_ref[...]
        for k in range(3):
            count = counts_ref[row, k * step_left + l * step_right]
            total = total + count * product[k * rows : (k + 1) * rows]
        total_ref[...] = total


def split(counts_ref, row, step_own, step_halo, aux_of, l):
    total = None
    for k in range(3):
        part = counts_ref[row, k * step_own + l * step_halo] * aux_of(k).astype(F32)
        total = part if total is None else total + part
    high = total.astype(jnp.bfloat16)
    return high, (total - high.astype(F32)).astype(jnp.bfloat16)


def fill(counts_ref, row, step_own, step_halo, source, store):
    rows = BLOCK

    def one(n, carry):
        l, r = n // (rows // 32), pl.multiple_of(n % (rows // 32) * 32, 32)
        high, low = split(counts_ref, row, step_own, step_halo, lambda k: source(k, r), l)
        store(l, r, high)
        store(l, rows + r, low)
        return carry

    lax.fori_loop(0, 3 * rows // 32, one, 0)


def store_columns(early, early_ref, late_ref):
    def store(l, r, values):
        early_ref[l, pl.ds(r, 32)] = values[:, :early]
        late_ref[l, pl.ds(r, 32)] = values[:, early:]

    return store


def edge_kernel(meta_ref, counts_ref, own_hbm, mix_early, mix_late, mix_far, own_ref, sem):
    live, even = meta_ref[0, 0], meta_ref[0, 1] == 1
    copy = pltpu.make_async_copy(own_hbm.at[meta_ref[0, 2]], own_ref, sem)
    copy.start()
    step_own = jnp.where(even, 1, 3)
    step_halo = jnp.where(even, 3, 1)
    early = mix_early.shape[-1]
    copy.wait()

    def far_store(l, r, values):
        mix_far[l, pl.ds(r, 32)] = values

    row_adj = jnp.where(even, 2, live * 2 + 2)
    row_far = jnp.where(even, 1, live * 2 + 3)
    store = store_columns(early, mix_early, mix_late)
    fill(counts_ref, row_adj, step_own, step_halo, lambda k, r: own_ref[k, pl.ds(r, 32)], store)
    fill(counts_ref, row_far, step_own, step_halo, lambda k, r: own_ref[k, pl.ds(r, 32), early:], far_store)


def edge_part(meta, counts, own):
    cap, aux, rows, width = own.shape
    late = width - EARLY
    smem = pl.BlockSpec(memory_space=pltpu.SMEM)
    vmem = pl.BlockSpec(memory_space=pltpu.VMEM)
    return pl.pallas_call(
        edge_kernel,
        in_specs=[smem, smem, pl.BlockSpec(memory_space=pltpu.HBM)],
        out_specs=(vmem,) * 3,
        scratch_shapes=[pltpu.VMEM((aux, rows, width), own.dtype), pltpu.SemaphoreType.DMA(())],
        out_shape=tuple(pltpu.VMEM((aux, 2 * rows, size), own.dtype) for size in (EARLY, late, late)),
        compiler_params=pltpu.CompilerParams(vmem_limit_bytes=EARLY_LIMIT),
        name="edge_mix",
        cost_estimate=pl.CostEstimate(flops=30_000_000, bytes_accessed=10_000_000, transcendentals=0),
    )(meta, counts, in_hbm(own))


def main_kernel(
    meta_ref, counts_ref, own_hbm, partner_hbm, after, sum_ref, back_ref, mix_early, mix_late,
    own_ref, inner_ref, edge_ref, sems
):
    del after
    live, even = meta_ref[0, 0], meta_ref[0, 1] == 1
    sec_out, adjacent, second = meta_ref[0, 3], meta_ref[0, 4], meta_ref[0, 5]
    step_own = jnp.where(even, 3, 1)
    step_halo = jnp.where(even, 1, 3)
    _, _, rows, width = own_ref.shape

    def own_copy(s):
        return pltpu.make_async_copy(own_hbm.at[s], own_ref.at[s], sems.at[s])

    inner_copy = pltpu.make_async_copy(partner_hbm.at[meta_ref[0, 6]], inner_ref.at[0], sems.at[3])
    second_copy = pltpu.make_async_copy(partner_hbm.at[1], inner_ref.at[1], sems.at[4])
    for s in range(3):
        pl.when(s < live)(own_copy(s).start)
        if s == 0:
            pl.when(live < 3)(inner_copy.start)
            pl.when(live == 1)(second_copy.start)
    back_ref[...] = jnp.zeros_like(back_ref)

    def diag(s, carry):
        @pl.when(s < live)
        def _():
            own_copy(s).wait()
            total = dot_rows(own_ref[s, 0], own_ref[s, 0])
            for k in range(1, 3):
                total = total + dot_rows(own_ref[s, k], own_ref[s, k])
            sum_ref[s] = total

        @pl.when(s >= live)
        def _():
            sum_ref[s] = jnp.zeros((rows, rows), F32)

        return carry

    lax.fori_loop(0, 3, diag, 0)

    def own_edge(e, carry):
        i, j = e // 2, jnp.minimum(e + 1, 2)
        theirs = (live == 3) & (e == jnp.where(even, 2, 0))

        @pl.when((j < live) & jnp.logical_not(theirs))
        def _():
            row = (i + 2) * 2 + (j - i - 1)
            edge_ref[...] = jnp.zeros_like(edge_ref)
            weigh(counts_ref, row, 3, 1, flat(own_ref[i]), lambda l: own_ref[j, l], edge_ref)
            sum_ref[i] += edge_ref[...]
            sum_ref[j] += edge_ref[...].T

        return carry

    lax.fori_loop(0, 3, own_edge, 0)
    pl.when(live < 3)(inner_copy.wait)
    pl.when(live == 1)(second_copy.wait)
    half = width // 2

    def inner_edge(t, carry):
        e, side = t // 2, t % 2
        mine = (live == 1) | ((live == 2) & ((e == 1) | (side == jnp.where(even, 0, 1))))

        @pl.when(mine)
        def _():
            slot = jnp.where(e == 0, adjacent, second)
            halo = jnp.where((live == 1) & (e == 1), 1, 0)
            row_one = jnp.where(live == 1, jnp.where(even, 5, 1), jnp.where(even, live * 2 + 1, 3))
            row = jnp.where(e == 0, jnp.where(even, live * 2 + 2, 2), row_one)
            columns = pl.ds(pl.multiple_of(side * half, half), half)
            edge_ref[...] = jnp.zeros_like(edge_ref)
            weigh(
                counts_ref,
                row,
                step_own,
                step_halo,
                flat(own_ref[slot, :, :, columns]),
                lambda l: inner_ref[halo, l, :, columns],
                edge_ref,
            )
            sum_ref[slot] += edge_ref[...]
            back_ref[halo] += edge_ref[...].T

        return carry

    lax.fori_loop(0, 4, inner_edge, 0)

    @pl.when(live == 1)
    def _():
        row = jnp.where(even, 6, 0)
        edge_ref[...] = jnp.zeros_like(edge_ref)
        weigh(counts_ref, row, step_own, step_halo, flat(inner_ref[0]), lambda l: inner_ref[1, l], edge_ref)
        back_ref[0] += edge_ref[...]
        back_ref[1] += edge_ref[...].T

    early = mix_early.shape[-1]

    def put(source):
        row = jnp.where(even, 3, live * 2 + 1)
        fill(counts_ref, row, step_halo, step_own, source, store_columns(early, mix_early, mix_late))

    pl.when(live >= 2)(lambda: put(lambda k, r: own_ref[sec_out, k, pl.ds(r, 32)]))
    pl.when(live == 1)(lambda: put(lambda k, r: inner_ref[0, k, pl.ds(r, 32)]))


def main_part(meta, counts, own, partner, after):
    cap, aux, rows, width = own.shape
    late = width - EARLY
    smem = pl.BlockSpec(memory_space=pltpu.SMEM)
    vmem = pl.BlockSpec(memory_space=pltpu.VMEM)
    hbm = pl.BlockSpec(memory_space=pltpu.HBM)
    free = pl.BlockSpec(memory_space=pl.ANY)
    return pl.pallas_call(
        main_kernel,
        in_specs=[smem, smem, hbm, free, free],
        out_specs=(vmem,) * 4,
        scratch_shapes=[
            pltpu.VMEM((cap, aux, rows, width), own.dtype),
            pltpu.VMEM((2, aux, rows, width), own.dtype),
            pltpu.VMEM((rows, rows), F32),
            pltpu.SemaphoreType.DMA((5,)),
        ],
        out_shape=(
            jax.ShapeDtypeStruct((cap, rows, rows), F32),
            jax.ShapeDtypeStruct((2, rows, rows), F32),
            pltpu.VMEM((aux, 2 * rows, EARLY), own.dtype),
            pltpu.VMEM((aux, 2 * rows, late), own.dtype),
        ),
        compiler_params=pltpu.CompilerParams(vmem_limit_bytes=MAIN_LIMIT),
        name="own_and_inner",
        cost_estimate=pl.CostEstimate(
            flops=50 * 2 * rows * rows * width, bytes_accessed=16_000_000, transcendentals=0
        ),
    )(meta, counts, in_hbm(own), partner, after)


def mixed(mix_ref, right_of):
    total = None
    for l in range(3):
        part = dot_rows(mix_ref[l], right_of(l))
        total = part if total is None else total + part
    rows = total.shape[1]
    return total[:rows] + total[rows:]


def early_kernel(mix_ref, outer_ref, back_ref, sec_ref):
    sec = mixed(mix_ref, lambda l: outer_ref[l])
    back_ref[...] = sec.T
    sec_ref[...] = sec


def early_part(mix, outer):
    aux, rows, width = outer.shape
    vmem = pl.BlockSpec(memory_space=pltpu.VMEM)
    return pl.pallas_call(
        early_kernel,
        in_specs=[vmem] * 2,
        out_specs=(vmem,) * 2,
        out_shape=(jax.ShapeDtypeStruct((rows, rows), F32),) * 2,
        compiler_params=pltpu.CompilerParams(vmem_limit_bytes=EARLY_LIMIT),
        name="outer_early",
        cost_estimate=pl.CostEstimate(
            flops=6 * 2 * rows * rows * width, bytes_accessed=1_000_000, transcendentals=0
        ),
    )(mix, outer)


def adjacent_kernel(mix_ref, outer_ref, adj_ref):
    adj_ref[...] = mixed(mix_ref, lambda l: outer_ref[l])


def adjacent_part(mix, outer):
    aux, rows, width = outer.shape
    vmem = pl.BlockSpec(memory_space=pltpu.VMEM)
    return pl.pallas_call(
        adjacent_kernel,
        in_specs=[vmem] * 2,
        out_specs=vmem,
        out_shape=jax.ShapeDtypeStruct((rows, rows), F32),
        compiler_params=pltpu.CompilerParams(vmem_limit_bytes=EARLY_LIMIT),
        name="outer_adjacent",
        cost_estimate=pl.CostEstimate(
            flops=6 * 2 * rows * rows * width, bytes_accessed=1_000_000, transcendentals=0
        ),
    )(mix, outer)


def late_kernel(
    meta_ref, adj_mix, sec_mix, far_mix, outer_ref, adj_in, sec_in, inner_in, adj_ref, sec_ref, *inner_refs
):
    sec = sec_in[...] + mixed(sec_mix, lambda l: outer_ref[0, l])
    adj = mixed(adj_mix, lambda l: outer_ref[0, l]) + mixed(far_mix, lambda l: outer_ref[1, l])
    near = inner_in[0] + jnp.where(meta_ref[0, 0] == 1, sec, 0.0)
    half = near.shape[0] // 2
    inner_refs[0][...] = near[:half]
    inner_refs[1][...] = near[half:]
    inner_refs[2][...] = inner_in[1, :half]
    inner_refs[3][...] = inner_in[1, half:]
    sec_ref[...] = sec
    adj_ref[...] = adj_in[...] + adj


def late_part(meta, mixes, outer, adj, sec, inner_back):
    _, aux, rows, width = outer.shape
    square = jax.ShapeDtypeStruct((rows, rows), F32)
    vmem = pl.BlockSpec(memory_space=pltpu.VMEM)
    return pl.pallas_call(
        late_kernel,
        in_specs=[pl.BlockSpec(memory_space=pltpu.SMEM)] + [vmem] * 7,
        out_specs=(vmem,) * 6,
        out_shape=(square, square) + (jax.ShapeDtypeStruct((rows // 2, rows), F32),) * 4,
        compiler_params=pltpu.CompilerParams(vmem_limit_bytes=LATE_LIMIT),
        name="outer_late",
        cost_estimate=pl.CostEstimate(
            flops=18 * 2 * rows * rows * width, bytes_accessed=1_000_000, transcendentals=0
        ),
    )(meta, *mixes, outer, adj, sec, inner_back)


def settle_kernel(meta_ref, sum_ref, adj_ref, sec_ref, out_ref):
    out_ref[...] = sum_ref[...]
    out_ref[meta_ref[0, 2]] += adj_ref[...]

    @pl.when(meta_ref[0, 0] >= 2)
    def _():
        out_ref[meta_ref[0, 3]] += sec_ref[...]


def finish_kernel(meta_ref, sum_ref, outer_ref, near_top, near_low, next_top, next_low, out_ref):
    out_ref[...] = sum_ref[...]
    out_ref[meta_ref[0, 2]] += outer_ref[...]
    half = near_top.shape[0]
    out_ref[meta_ref[0, 4], :half] += near_top[...]
    out_ref[meta_ref[0, 4], half:] += near_low[...]
    out_ref[meta_ref[0, 5], :half] += next_top[...]
    out_ref[meta_ref[0, 5], half:] += next_low[...]


def add_blocks(kernel, name, meta, total, *blocks):
    vmem = pl.BlockSpec(memory_space=pltpu.VMEM)
    return pl.pallas_call(
        kernel,
        in_specs=[pl.BlockSpec(memory_space=pltpu.SMEM)] + [vmem] * (1 + len(blocks)),
        out_specs=vmem,
        out_shape=jax.ShapeDtypeStruct(total.shape, F32),
        compiler_params=pltpu.CompilerParams(vmem_limit_bytes=LATE_LIMIT),
        name=name,
        cost_estimate=pl.CostEstimate(flops=200_000, bytes_accessed=2_000_000, transcendentals=0),
    )(meta, total, *blocks)


def per_device(own, block_slot, pair_list, domain_slots):
    cap = own.shape[0]
    count = lax.axis_size("blk")
    me = lax.axis_index("blk")
    to_outer = [(d, d - 1) for d in range(2, count, 2)] + [(d, d + 1) for d in range(1, count - 1, 2)]
    to_inner = [(d, d ^ 1) for d in range(count)]
    outer_early = lax.ppermute(pick_early(me, block_slot, own), "blk", to_outer)
    partner = lax.ppermute(own, "blk", to_inner)
    counts, meta = pair_counts(me, block_slot, pair_list, domain_slots, cap)
    adj_early, adj_late, mix_far = edge_part(meta, counts, own)
    late_piece, token = pick_late(me, block_slot, own, partner, mix_far)
    outer_late = lax.ppermute(late_piece, "blk", to_outer)
    own_sum, inner_back, sec_early, sec_late = main_part(meta, counts, own, partner, token)
    outer_back, sec = early_part(sec_early, outer_early)
    from_outer = lax.ppermute(outer_back, "blk", to_outer)
    adj = adjacent_part(adj_early, outer_early)
    adj, sec, *backs = late_part(meta, (adj_late, sec_late, mix_far), outer_late, adj, sec, inner_back)
    from_inner = [lax.ppermute(piece, "blk", to_inner) for piece in backs]
    total = add_blocks(settle_kernel, "settle", meta, own_sum, adj, sec)
    return add_blocks(finish_kernel, "finish", meta, total, from_outer, *from_inner)


def solution(mesh):
    placed = (P("blk", None, None, None), P(), P(), P())
    return jax.shard_map(
        per_device, mesh=mesh, in_specs=placed, out_specs=P("blk", None, None), check_vma=False
    )
```

time: 62.8 us -> 57.7 us (0.919)
  Pallas kernels: 36.6 us -> 32.5 us
  local copies, waits for them, and re-layouts: 1.31 us -> 0.01 us
  waiting for transfers between devices: 10.9 us -> 12.2 us
  starting transfers between devices: 13.5 us -> 12.5 us
    ppermute x1, waiting for transfers between devices: 8.14 us -> 1.94 us  [per_device(): from_outer = lax.ppermute(outer_back, 'blk', to_outer)]
    ppermute x2 -> x5, waiting for transfers between devices: 0.01 us -> 6.08 us  [the longest x1 6.07 us: per_device(): outer_early = lax.ppermute(pick_early(me, block_slot, own), 'blk', to_outer)]
    pallas_call x4 -> x6, Pallas kernels: 30.2 us -> 27 us  [the longest x1 13.9 us: main_part(): pl.pallas_call(main_kernel, in_specs=[smem, smem, hbm, free, free], out_s...]
    ppermute x1, waiting for transfers between devices: 0.01 us -> 2.08 us  [per_device(): partner = lax.ppermute(own, 'blk', to_inner)]
    ppermute x1, starting transfers between devices: 6.77 us -> 4.7 us  [per_device(): outer_late = lax.ppermute(late_piece, 'blk', to_outer)]
    unnamed x4 -> x6, local copies, waits for them, and re-layouts: 1.31 us -> 0.01 us
    ppermute x2 -> x5, starting transfers between devices: 3.09 us -> 4.11 us  [the longest x1 3.02 us: per_device(): outer_early = lax.ppermute(pick_early(me, block_slot, own), 'blk', to_outer)]
    pallas_call x1, Pallas kernels: 2.62 us -> 1.68 us  [early_part(): pl.pallas_call(early_kernel, in_specs=[vmem] * 2, out_specs=(vmem,) * 2,...]
  transfers between devices with their start and end apart: 5 -> 8, of which waited for: 2 -> 4; matrix products, arithmetic and copies ran while one was open for 0% -> 0% of each run, Pallas kernels for 53% -> 54%
where the time goes in v2:
time: 57.7 us; the launch traced here: 57.3 us
  Pallas kernels  32.5 us (56%)
  starting transfers between devices  12.5 us (22%)
  waiting for transfers between devices  12.2 us (21%)
    pallas_call x1, Pallas kernels, main_part(): pl.pallas_call(main_kernel, in_specs=[smem, smem, hbm, free, free], out_s...  13.9 us
    ppermute x1, waiting for transfers between devices, per_device(): outer_early = lax.ppermute(pick_early(me, block_slot, own), 'blk', to_outer)  6.07 us
    pallas_call x1, Pallas kernels, edge_part(): pl.pallas_call(edge_kernel, in_specs=[smem, smem, pl.BlockSpec(memory_spa...  5.9 us
    pallas_call x2, Pallas kernels, pick_call(): pl.pallas_call(kernel, out_shape=(pltpu.VMEM(shape, blocks[0].dtype),) +...  4.8 us
    ppermute x1, starting transfers between devices, per_device(): outer_late = lax.ppermute(late_piece, 'blk', to_outer)  4.7 us
    ppermute x1, starting transfers between devices, per_device(): from_outer = lax.ppermute(outer_back, 'blk', to_outer)  3.02 us
    ppermute x1, starting transfers between devices, per_device(): outer_early = lax.ppermute(pick_early(me, block_slot, own), 'blk', to_outer)  3.02 us
    pallas_call x2, Pallas kernels, add_blocks(): pl.pallas_call(kernel, in_specs=[pl.BlockSpec(memory_space=pltpu.SMEM)] +...  2.33 us
  transfers between devices with their start and end apart: 8, of which 4 were waited for; matrix products, arithmetic and copies ran while one was open for 0% of the time, Pallas kernels for 54%

profile of v2, /device:TPU:63, one launch (start us, length us, event | category | flops | bytes accessed | tf_op | source)
XLA Modules:
  0.0 57.3 jit_solution(12172891429534269259)
XLA Ops:
  0.0 0.7 %collective-permute-start = (bf16[3,3,256,2048]{3,2,1,0:T(8,128)(2,1)}, bf16[3,3,256,2048]{3,2,1,0:T(8,128)(2,1)}, u32[]{:S(2)}, u32[]{:S(2)}) collective-permute-start(bf16[3,3,256,2048]{3,2,1,0:T(8,128)(2,1)} %own_ref.3), channel_id=1, source_target_pairs={{0,1},{1,0},{2,3},{3,2},{4,5},{5,4},{6,7},{7,6},{8,9},{9,8},{10,11... | collective-permute-start | bytes 28311560 | tf_op jit(solution)/shard_map/ppermute | solution.py:502
  0.7 2.8 %pick.1 = bf16[3,256,1792]{2,1,0:T(8,128)(2,1)S(1)} custom-call(s32[1]{0:T(128)} %bitcast.me_ref, s32[256]{0:T(256)} %slots_ref.5, bf16[3,3,256,2048]{3,2,1,0:T(8,128)(2,1)} %own_ref.3), custom_call_target="tpu_custom_call" | custom-call | bytes 5505024 | tf_op jit(solution)/shard_map/pick/pallas_call | solution.py:89
  3.5 3.0 %collective-permute-start.2 = (bf16[3,256,1792]{2,1,0:T(8,128)(2,1)S(1)}, bf16[3,256,1792]{2,1,0:T(8,128)(2,1)S(1)}, u32[]{:S(2)}, u32[]{:S(2)}) collective-permute-start(bf16[3,256,1792]{2,1,0:T(8,128)(2,1)S(1)} %pick.1), channel_id=1, source_target_pairs={{2,1},{4,3},{6,5},{8,7},{10,9},{12,11},{14,13},{16,15},{18,17},{20... | collective-permute-start | bytes 8257544 | tf_op jit(solution)/shard_map/ppermute | solution.py:501
  6.5 0.8 %pair_counts.1 = (f32[16,16]{1,0:T(8,128)S(1)}, s32[8,128]{1,0:T(8,128)S(1)}) custom-call(s32[1]{0:T(128)} %bitcast.me_ref, s32[256]{0:T(256)S(1)} %copy-done.2, s32[2,6144]{1,0:T(2,128)S(1)} %bitcast.4, s32[4,6144]{1,0:T(4,128)S(1)} %bitcast.3), custom_call_target="tpu_custom_call" | custom-call | flops 4000000 | bytes 200000 | tf_op jit(solution)/shard_map/pair_counts/pallas_call | solution.py:155
  7.3 5.9 %edge_mix.1 = (bf16[3,512,1792]{2,1,0:T(8,128)(2,1)S(1)}, bf16[3,512,256]{2,1,0:T(8,128)(2,1)S(1)}, bf16[3,512,256]{2,1,0:T(8,128)(2,1)S(1)}) custom-call(s32[8,128]{1,0:T(8,128)S(1)} %get-tuple-element.24.meta_ref, f32[16,16]{1,0:T(8,128)S(1)} %get-tuple-element.25.counts_ref, bf16[3,3,256,2048]{3,2,1,0:T(8,128)(2,1)} %own_ref.3), custom_call_target="tpu_custom_call" | custom-call | flops 30000000 | bytes 10000000 | tf_op jit(solution)/shard_map/edge_mix/pallas_call | solution.py:232
  13.2 2.1 %collective-permute-done.partner_ref.partner_hbm = bf16[3,3,256,2048]{3,2,1,0:T(8,128)(2,1)} collective-permute-done((bf16[3,3,256,2048]{3,2,1,0:T(8,128)(2,1)}, bf16[3,3,256,2048]{3,2,1,0:T(8,128)(2,1)}, u32[]{:S(2)}, u32[]{:S(2)}) %collective-permute-start) | collective-permute-done | bytes 9437216 | tf_op jit(solution)/shard_map/ppermute | solution.py:502
  15.3 2.0 %pick_two.1 = (bf16[2,3,256,256]{3,2,1,0:T(8,128)(2,1)S(1)}, f32[8,128]{1,0:T(8,128)S(1)}) custom-call(s32[1]{0:T(128)} %bitcast.me_ref, s32[256]{0:T(256)} %slots_ref.5, bf16[3,3,256,2048]{3,2,1,0:T(8,128)(2,1)} %own_ref.3, bf16[3,3,256,2048]{3,2,1,0:T(8,128)(2,1)} %collective-permute-done.partner_ref.partner_hbm, ...), custom_call_target="tpu_custom_call" | custom-call | bytes 1572864 | tf_op jit(solution)/shard_map/pick_two/pallas_call | solution.py:89
  17.3 4.7 %collective-permute-start.1 = (bf16[2,3,256,256]{3,2,1,0:T(8,128)(2,1)S(1)}, bf16[2,3,256,256]{3,2,1,0:T(8,128)(2,1)S(1)}, u32[]{:S(2)}, u32[]{:S(2)}) collective-permute-start(bf16[2,3,256,256]{3,2,1,0:T(8,128)(2,1)S(1)} %get-tuple-element.31), channel_id=1, source_target_pairs={{2,1},{4,3},{6,5},{8,7},{10,9},{12,11},{14,13},{16,15},{18,17},{20... | collective-permute-start | bytes 2359304 | tf_op jit(solution)/shard_map/ppermute | solution.py:506
  22.0 13.9 %own_and_inner.1 = (f32[3,256,256]{2,1,0:T(8,128)S(1)}, f32[2,256,256]{2,1,0:T(8,128)S(1)}, bf16[3,512,1792]{2,1,0:T(8,128)(2,1)S(1)}, bf16[3,512,256]{2,1,0:T(8,128)(2,1)S(1)}) custom-call(s32[8,128]{1,0:T(8,128)S(1)} %get-tuple-element.24.meta_ref, f32[16,16]{1,0:T(8,128)S(1)} %get-tuple-element.25.counts_ref, bf16[3,3,256,2048]{3,2,1,0:T(8,128)(2,1)} %own_ref.3, ...), custom_call_target="tpu_custom_call" | custom-call | flops 13421772800 | bytes 16000000 | tf_op jit(solution)/shard_map/own_and_inner/pallas_call | solution.py:356
  36.0 6.1 %collective-permute-done.2.outer_ref = bf16[3,256,1792]{2,1,0:T(8,128)(2,1)S(1)} collective-permute-done((bf16[3,256,1792]{2,1,0:T(8,128)(2,1)S(1)}, bf16[3,256,1792]{2,1,0:T(8,128)(2,1)S(1)}, u32[]{:S(2)}, u32[]{:S(2)}) %collective-permute-start.2) | collective-permute-done | bytes 2752544 | tf_op jit(solution)/shard_map/ppermute | solution.py:501
  42.1 1.7 %outer_early.1 = (f32[256,256]{1,0:T(8,128)S(1)}, f32[256,256]{1,0:T(8,128)S(1)}) custom-call(bf16[3,512,1792]{2,1,0:T(8,128)(2,1)S(1)} %get-tuple-element.33.mix_ref, bf16[3,256,1792]{2,1,0:T(8,128)(2,1)S(1)} %collective-permute-done.2.outer_ref), custom_call_target="tpu_custom_call" | custom-call | flops 1409286144 | bytes 1000000 | tf_op jit(solution)/shard_map/outer_early/pallas_call | solution.py:398
  43.7 3.0 %collective-permute-start.3 = (f32[256,256]{1,0:T(8,128)S(1)}, f32[256,256]{1,0:T(8,128)S(1)}, u32[]{:S(2)}, u32[]{:S(2)}) collective-permute-start(f32[256,256]{1,0:T(8,128)S(1)} %get-tuple-element.38), channel_id=1, source_target_pairs={{2,1},{4,3},{6,5},{8,7},{10,9},{12,11},{14,13},{16,15},{18,17},{20... | collective-permute-start | bytes 786440 | tf_op jit(solution)/shard_map/ppermute | solution.py:509
  46.8 1.6 %outer_adjacent.1.adj_in = f32[256,256]{1,0:T(8,128)S(1)} custom-call(bf16[3,512,1792]{2,1,0:T(8,128)(2,1)S(1)} %get-tuple-element.32.mix_ref, bf16[3,256,1792]{2,1,0:T(8,128)(2,1)S(1)} %collective-permute-done.2.outer_ref), custom_call_target="tpu_custom_call" | custom-call | flops 1409286144 | bytes 1000000 | tf_op jit(solution)/shard_map/outer_adjacent/pallas_call | solution.py:418
  48.4 2.1 %collective-permute-done.1.outer_ref = bf16[2,3,256,256]{3,2,1,0:T(8,128)(2,1)S(1)} collective-permute-done((bf16[2,3,256,256]{3,2,1,0:T(8,128)(2,1)S(1)}, bf16[2,3,256,256]{3,2,1,0:T(8,128)(2,1)S(1)}, u32[]{:S(2)}, u32[]{:S(2)}) %collective-permute-start.1) | collective-permute-done | bytes 786464 | tf_op jit(solution)/shard_map/ppermute | solution.py:506
  50.5 1.4 %outer_late.1 = (f32[256,256]{1,0:T(8,128)S(1)}, f32[256,256]{1,0:T(8,128)S(1)}, f32[128,256]{1,0:T(8,128)S(1)}, f32[128,256]{1,0:T(8,128)S(1)}, f32[128,256]{1,0:T(8,128)S(1)}, /*index=5*/f32[128,256]{1,0:T(8,128)S(1)}) custom-call(s32[8,128]{1,0:T(8,128)S(1)} %get-tuple-element.24.meta_ref, bf16[3,512,256]{2,1,0:T(8,128)(2,1)S(1)} %get-tuple-element.29.adj_mix, ...), custom_call_target="tpu_custom_call" | custom-call | flops 603979776 | bytes 1000000 | tf_op jit(solution)/shard_map/outer_late/pallas_call | solution.py:450
  51.9 0.1 collective-permute-start.4
  52.0 0.5 collective-permute-start.5
  52.5 0.1 collective-permute-start.6
  52.6 0.4 collective-permute-start.7
  53.0 0.7 %settle.1.sum_ref = f32[3,256,256]{2,1,0:T(8,128)S(1)} custom-call(s32[8,128]{1,0:T(8,128)S(1)} %get-tuple-element.24.meta_ref, f32[3,256,256]{2,1,0:T(8,128)S(1)} %get-tuple-element.28.sum_ref, f32[256,256]{1,0:T(8,128)S(1)} %get-tuple-element.36.adj_ref, f32[256,256]{1,0:T(8,128)S(1)} %get-tuple-element.37.sec_ref), custom_call_target="tpu_custom_call" | custom-call | flops 200000 | bytes 2000000 | tf_op jit(solution)/shard_map/settle/pallas_call | solution.py:484
  53.7 1.9 %collective-permute-done.3.outer_ref = f32[256,256]{1,0:T(8,128)S(1)} collective-permute-done((f32[256,256]{1,0:T(8,128)S(1)}, f32[256,256]{1,0:T(8,128)S(1)}, u32[]{:S(2)}, u32[]{:S(2)}) %collective-permute-start.3) | collective-permute-done | bytes 262176 | tf_op jit(solution)/shard_map/ppermute | solution.py:509
  55.7 0.0 collective-permute-done.4.near_top
  55.7 0.0 collective-permute-done.5.near_low
  55.7 1.6 %finish.1 = f32[3,256,256]{2,1,0:T(8,128)} custom-call(s32[8,128]{1,0:T(8,128)S(1)} %get-tuple-element.24.meta_ref, f32[3,256,256]{2,1,0:T(8,128)S(1)} %settle.1.sum_ref, f32[256,256]{1,0:T(8,128)S(1)} %collective-permute-done.3.outer_ref, f32[128,256]{1,0:T(8,128)S(1)} %collective-permute-done.4.near_top, f32[128,256]{1,0:T(8,128)S(1)} %collective-permute-done.5.near_low, ...), custom_call_target="tpu_custom_call" | custom-call | flops 200000 | bytes 2000000 | tf_op jit(solution)/shard_map/finish/pallas_call | solution.py:484
  (8 shorter events, 0.0 us)
Async XLA Ops:
  0.0 15.3 %collective-permute-start = (bf16[3,3,256,2048]{3,2,1,0:T(8,128)(2,1)}, bf16[3,3,256,2048]{3,2,1,0:T(8,128)(2,1)}, u32[]{:S(2)}, u32[]{:S(2)}) collective-permute-start(bf16[3,3,256,2048]{3,2,1,0:T(8,128)(2,1)} %own_ref.3), channel_id=1, source_target_pairs={{0,1},{1,0},{2,3},{3,2},{4,5},{5,4},{6,7},{7,6},{8,9},{9,8},{10,11... | collective-permute-start | bytes 28311560 | tf_op jit(solution)/shard_map/ppermute | solution.py:502
  0.7 5.8 %copy-start = (s32[6144,4]{0,1:T(4,128)S(1)}, s32[6144,4]{0,1:T(4,128)}, u32[]{:S(2)}) copy-start(s32[6144,4]{0,1:T(4,128)} %param.7) | copy-start | bytes 294916
  0.7 5.8 %copy-start.1 = (s32[6144,2]{0,1:T(2,128)S(1)}, s32[6144,2]{0,1:T(2,128)}, u32[]{:S(2)}) copy-start(s32[6144,2]{0,1:T(2,128)} %param.6) | copy-start | bytes 147460
  0.7 5.8 %copy-start.2 = (s32[256]{0:T(256)S(1)}, s32[256]{0:T(256)}, u32[]{:S(2)}) copy-start(s32[256]{0:T(256)} %slots_ref.5) | copy-start | bytes 3076
  3.5 38.6 %collective-permute-start.2 = (bf16[3,256,1792]{2,1,0:T(8,128)(2,1)S(1)}, bf16[3,256,1792]{2,1,0:T(8,128)(2,1)S(1)}, u32[]{:S(2)}, u32[]{:S(2)}) collective-permute-start(bf16[3,256,1792]{2,1,0:T(8,128)(2,1)S(1)} %pick.1), channel_id=1, source_target_pairs={{2,1},{4,3},{6,5},{8,7},{10,9},{12,11},{14,13},{16,15},{18,17},{20... | collective-permute-start | bytes 8257544 | tf_op jit(solution)/shard_map/ppermute | solution.py:501
  17.3 33.2 %collective-permute-start.1 = (bf16[2,3,256,256]{3,2,1,0:T(8,128)(2,1)S(1)}, bf16[2,3,256,256]{3,2,1,0:T(8,128)(2,1)S(1)}, u32[]{:S(2)}, u32[]{:S(2)}) collective-permute-start(bf16[2,3,256,256]{3,2,1,0:T(8,128)(2,1)S(1)} %get-tuple-element.31), channel_id=1, source_target_pairs={{2,1},{4,3},{6,5},{8,7},{10,9},{12,11},{14,13},{16,15},{18,17},{20... | collective-permute-start | bytes 2359304 | tf_op jit(solution)/shard_map/ppermute | solution.py:506
  43.7 11.9 %collective-permute-start.3 = (f32[256,256]{1,0:T(8,128)S(1)}, f32[256,256]{1,0:T(8,128)S(1)}, u32[]{:S(2)}, u32[]{:S(2)}) collective-permute-start(f32[256,256]{1,0:T(8,128)S(1)} %get-tuple-element.38), channel_id=1, source_target_pairs={{2,1},{4,3},{6,5},{8,7},{10,9},{12,11},{14,13},{16,15},{18,17},{20... | collective-permute-start | bytes 786440 | tf_op jit(solution)/shard_map/ppermute | solution.py:509
  51.9 3.8 %collective-permute-start.4 = (f32[128,256]{1,0:T(8,128)S(1)}, f32[128,256]{1,0:T(8,128)S(1)}, u32[]{:S(2)}, u32[]{:S(2)}) collective-permute-start(f32[128,256]{1,0:T(8,128)S(1)} %get-tuple-element.39), channel_id=1, source_target_pairs={{0,1},{1,0},{2,3},{3,2},{4,5},{5,4},{6,7},{7,6},{8,9},{9,8},{10,11... | collective-permute-start | bytes 393224 | tf_op jit(solution)/shard_map/ppermute | solution.py:512
  52.0 3.7 %collective-permute-start.5 = (f32[128,256]{1,0:T(8,128)S(1)}, f32[128,256]{1,0:T(8,128)S(1)}, u32[]{:S(2)}, u32[]{:S(2)}) collective-permute-start(f32[128,256]{1,0:T(8,128)S(1)} %get-tuple-element.40), channel_id=1, source_target_pairs={{0,1},{1,0},{2,3},{3,2},{4,5},{5,4},{6,7},{7,6},{8,9},{9,8},{10,11... | collective-permute-start | bytes 393224 | tf_op jit(solution)/shard_map/ppermute | solution.py:512
  52.5 3.2 %collective-permute-start.6 = (f32[128,256]{1,0:T(8,128)S(1)}, f32[128,256]{1,0:T(8,128)S(1)}, u32[]{:S(2)}, u32[]{:S(2)}) collective-permute-start(f32[128,256]{1,0:T(8,128)S(1)} %get-tuple-element.41), channel_id=1, source_target_pairs={{0,1},{1,0},{2,3},{3,2},{4,5},{5,4},{6,7},{7,6},{8,9},{9,8},{10,11... | collective-permute-start | bytes 393224 | tf_op jit(solution)/shard_map/ppermute | solution.py:512
  52.6 3.1 %collective-permute-start.7 = (f32[128,256]{1,0:T(8,128)S(1)}, f32[128,256]{1,0:T(8,128)S(1)}, u32[]{:S(2)}, u32[]{:S(2)}) collective-permute-start(f32[128,256]{1,0:T(8,128)S(1)} %get-tuple-element.42), channel_id=1, source_target_pairs={{0,1},{1,0},{2,3},{3,2},{4,5},{5,4},{6,7},{7,6},{8,9},{9,8},{10,11... | collective-permute-start | bytes 393224 | tf_op jit(solution)/shard_map/ppermute | solution.py:512

commit v3 on v2

--- a/solution.py
+++ b/solution.py
@@ -242,7 +242,7 @@
 
 
 def main_kernel(
-    meta_ref, counts_ref, own_hbm, partner_hbm, after, sum_ref, back_ref, mix_early, mix_late,
+    meta_ref, counts_ref, own_hbm, partner_hbm, after, sum_ref, near_ref, next_ref, mix_early, mix_late,
     own_ref, inner_ref, edge_ref, sems
 ):
     del after
@@ -262,7 +262,8 @@
         if s == 0:
             pl.when(live < 3)(inner_copy.start)
             pl.when(live == 1)(second_copy.start)
-    back_ref[...] = jnp.zeros_like(back_ref)
+    near_ref[...] = jnp.zeros_like(near_ref)
+    next_ref[...] = jnp.zeros_like(next_ref)
 
     def diag(s, carry):
         @pl.when(s < live)
@@ -322,7 +323,15 @@
                 edge_ref,
             )
             sum_ref[slot] += edge_ref[...]
-            back_ref[halo] += edge_ref[...].T
+
+            @pl.when(halo == 0)
+            def _():
+                near_ref[...] += edge_ref[...].T
+
+            @pl.when(halo == 1)
+            def _():
+                next_ref[...] += edge_ref[...].T
+
 
         return carry
 
@@ -333,8 +342,8 @@
         row = jnp.where(even, 6, 0)
         edge_ref[...] = jnp.zeros_like(edge_ref)
         weigh(counts_ref, row, step_own, step_halo, flat(inner_ref[0]), lambda l: inner_ref[1, l], edge_ref)
-        back_ref[0] += edge_ref[...]
-        back_ref[1] += edge_ref[...].T
+        near_ref[...] += edge_ref[...]
+        next_ref[...] += edge_ref[...].T
 
     early = mix_early.shape[-1]
 
@@ -356,7 +365,7 @@
     return pl.pallas_call(
         main_kernel,
         in_specs=[smem, smem, hbm, free, free],
-        out_specs=(vmem,) * 4,
+        out_specs=(vmem,) * 5,
         scratch_shapes=[
             pltpu.VMEM((cap, aux, rows, width), own.dtype),
             pltpu.VMEM((2, aux, rows, width), own.dtype),
@@ -365,7 +374,8 @@
         ],
         out_shape=(
             jax.ShapeDtypeStruct((cap, rows, rows), F32),
-            jax.ShapeDtypeStruct((2, rows, rows), F32),
+            jax.ShapeDtypeStruct((rows, rows), F32),
+            jax.ShapeDtypeStruct((rows, rows), F32),
             pltpu.VMEM((aux, 2 * rows, EARLY), own.dtype),
             pltpu.VMEM((aux, 2 * rows, late), own.dtype),
         ),
@@ -433,12 +443,10 @@
 ):
     sec = sec_in[...] + mixed(sec_mix, lambda l: outer_ref[0, l])
     adj = mixed(adj_mix, lambda l: outer_ref[0, l]) + mixed(far_mix, lambda l: outer_ref[1, l])
-    near = inner_in[0] + jnp.where(meta_ref[0, 0] == 1, sec, 0.0)
+    near = inner_in[...] + jnp.where(meta_ref[0, 0] == 1, sec, 0.0)
     half = near.shape[0] // 2
     inner_refs[0][...] = near[:half]
     inner_refs[1][...] = near[half:]
-    inner_refs[2][...] = inner_in[1, :half]
-    inner_refs[3][...] = inner_in[1, half:]
     sec_ref[...] = sec
     adj_ref[...] = adj_in[...] + adj
 
@@ -450,8 +458,8 @@
     return pl.pallas_call(
         late_kernel,
         in_specs=[pl.BlockSpec(memory_space=pltpu.SMEM)] + [vmem] * 7,
-        out_specs=(vmem,) * 6,
-        out_shape=(square, square) + (jax.ShapeDtypeStruct((rows // 2, rows), F32),) * 4,
+        out_specs=(vmem,) * 4,
+        out_shape=(square, square) + (jax.ShapeDtypeStruct((rows // 2, rows), F32),) * 2,
         compiler_params=pltpu.CompilerParams(vmem_limit_bytes=LATE_LIMIT),
         name="outer_late",
         cost_estimate=pl.CostEstimate(
@@ -460,36 +468,55 @@
     )(meta, *mixes, outer, adj, sec, inner_back)
 
 
-def settle_kernel(meta_ref, sum_ref, adj_ref, sec_ref, out_ref):
+def settle_kernel(meta_ref, sum_ref, adj_ref, sec_ref, next_ref, out_ref, place_ref):
     out_ref[...] = sum_ref[...]
+    out_ref[meta_ref[0, 5]] += next_ref[...]
     out_ref[meta_ref[0, 2]] += adj_ref[...]
 
     @pl.when(meta_ref[0, 0] >= 2)
     def _():
         out_ref[meta_ref[0, 3]] += sec_ref[...]
 
-
-def finish_kernel(meta_ref, sum_ref, outer_ref, near_top, near_low, next_top, next_low, out_ref):
-    out_ref[...] = sum_ref[...]
-    out_ref[meta_ref[0, 2]] += outer_ref[...]
+    row = lax.broadcasted_iota(jnp.int32, place_ref.shape, 0)
+    hit = (row == meta_ref[0, 2]) | (row == meta_ref[0, 4] + 3)
+    place_ref[...] = jnp.where(hit, 1.0, 0.0)
+
+
+def settle(meta, total, *blocks):
+    vmem = pl.BlockSpec(memory_space=pltpu.VMEM)
+    return pl.pallas_call(
+        settle_kernel,
+        in_specs=[pl.BlockSpec(memory_space=pltpu.SMEM)] + [vmem] * (1 + len(blocks)),
+        out_specs=(vmem, vmem),
+        out_shape=(pltpu.VMEM(total.shape, F32), pltpu.VMEM((8, total.shape[2]), F32)),
+        compiler_params=pltpu.CompilerParams(vmem_limit_bytes=LATE_LIMIT),
+        name="settle",
+        cost_estimate=pl.CostEstimate(flops=200_000, bytes_accessed=2_000_000, transcendentals=0),
+    )(meta, total, *blocks)
+
+
+def finish_kernel(place_ref, sum_ref, outer_ref, near_top, near_low, out_ref):
     half = near_top.shape[0]
-    out_ref[meta_ref[0, 4], :half] += near_top[...]
-    out_ref[meta_ref[0, 4], half:] += near_low[...]
-    out_ref[meta_ref[0, 5], :half] += next_top[...]
-    out_ref[meta_ref[0, 5], half:] += next_low[...]
-
-
-def add_blocks(kernel, name, meta, total, *blocks):
-    vmem = pl.BlockSpec(memory_space=pltpu.VMEM)
-    return pl.pallas_call(
-        kernel,
-        in_specs=[pl.BlockSpec(memory_space=pltpu.SMEM)] + [vmem] * (1 + len(blocks)),
+    for s in range(3):
+        for rows, near in ((slice(0, half), near_top), (slice(half, 2 * half), near_low)):
+            out_ref[s, rows] = (
+                sum_ref[s, rows]
+                + place_ref[s : s + 1] * outer_ref[rows]
+                + place_ref[3 + s : 4 + s] * near[...]
+            )
+
+
+def finish(place, total, *blocks):
+    vmem = pl.BlockSpec(memory_space=pltpu.VMEM)
+    return pl.pallas_call(
+        finish_kernel,
+        in_specs=[vmem] * (2 + len(blocks)),
         out_specs=vmem,
         out_shape=jax.ShapeDtypeStruct(total.shape, F32),
         compiler_params=pltpu.CompilerParams(vmem_limit_bytes=LATE_LIMIT),
-        name=name,
+        name="finish",
         cost_estimate=pl.CostEstimate(flops=200_000, bytes_accessed=2_000_000, transcendentals=0),
-    )(meta, total, *blocks)
+    )(place, total, *blocks)
 
 
 def per_device(own, block_slot, pair_list, domain_slots):
@@ -504,14 +531,15 @@
     adj_early, adj_late, mix_far = edge_part(meta, counts, own)
     late_piece, token = pick_late(me, block_slot, own, partner, mix_far)
     outer_late = lax.ppermute(late_piece, "blk", to_outer)
-    own_sum, inner_back, sec_early, sec_late = main_part(meta, counts, own, partner, token)
+    own_sum, inner_back, next_back, sec_early, sec_late = main_part(meta, counts, own, partner, token)
+    from_next = lax.ppermute(next_back, "blk", to_inner)
     outer_back, sec = early_part(sec_early, outer_early)
     from_outer = lax.ppermute(outer_back, "blk", to_outer)
     adj = adjacent_part(adj_early, outer_early)
     adj, sec, *backs = late_part(meta, (adj_late, sec_late, mix_far), outer_late, adj, sec, inner_back)
     from_inner = [lax.ppermute(piece, "blk", to_inner) for piece in backs]
-    total = add_blocks(settle_kernel, "settle", meta, own_sum, adj, sec)
-    return add_blocks(finish_kernel, "finish", meta, total, from_outer, *from_inner)
+    total, place = settle(meta, own_sum, adj, sec, from_next)
+    return finish(place, total, from_outer, *from_inner)
 
 
 def solution(mesh):

time: 57.7 us -> 57 us (0.988)
  Pallas kernels: 32.5 us -> 31.9 us
  transfers between devices with their start and end apart: 8 -> 7, of which waited for: 4 -> 4; matrix products, arithmetic and copies ran while one was open for 0% -> 0% of each run, Pallas kernels for 54% -> 54%
where the time goes in v3:
time: 57 us; the launch traced here: 56.7 us
  Pallas kernels  31.9 us (56%)
  waiting for transfers between devices  12.6 us (22%)
  starting transfers between devices  12.1 us (21%)
    pallas_call x1, Pallas kernels, main_part(): pl.pallas_call(main_kernel, in_specs=[smem, smem, hbm, free, free], out_s...  13.9 us
    ppermute x1, waiting for transfers between devices, per_device(): outer_early = lax.ppermute(pick_early(me, block_slot, own), 'blk', to_outer)  6.07 us
    pallas_call x1, Pallas kernels, edge_part(): pl.pallas_call(edge_kernel, in_specs=[smem, smem, pl.BlockSpec(memory_spa...  5.9 us
    pallas_call x2, Pallas kernels, pick_call(): pl.pallas_call(kernel, out_shape=(pltpu.VMEM(shape, blocks[0].dtype),) +...  4.8 us
    ppermute x1, starting transfers between devices, per_device(): outer_late = lax.ppermute(late_piece, 'blk', to_outer)  4.69 us
    ppermute x1, starting transfers between devices, per_device(): from_outer = lax.ppermute(outer_back, 'blk', to_outer)  3.02 us
    ppermute x1, starting transfers between devices, per_device(): outer_early = lax.ppermute(pick_early(me, block_slot, own), 'blk', to_outer)  3.02 us
    ppermute x1, waiting for transfers between devices, per_device(): from_outer = lax.ppermute(outer_back, 'blk', to_outer)  2.42 us
  transfers between devices with their start and end apart: 7, of which 4 were waited for; matrix products, arithmetic and copies ran while one was open for 0% of the time, Pallas kernels for 54%

profile of v3, /device:TPU:63, one launch (start us, length us, event | category | flops | bytes accessed | tf_op | source)
XLA Modules:
  0.0 56.7 jit_solution(11071236972518799357)
XLA Ops:
  0.0 0.7 %collective-permute-start = (bf16[3,3,256,2048]{3,2,1,0:T(8,128)(2,1)}, bf16[3,3,256,2048]{3,2,1,0:T(8,128)(2,1)}, u32[]{:S(2)}, u32[]{:S(2)}) collective-permute-start(bf16[3,3,256,2048]{3,2,1,0:T(8,128)(2,1)} %own_ref.3), channel_id=1, source_target_pairs={{0,1},{1,0},{2,3},{3,2},{4,5},{5,4},{6,7},{7,6},{8,9},{9,8},{10,11... | collective-permute-start | bytes 28311560 | tf_op jit(solution)/shard_map/ppermute | solution.py:529
  0.7 2.8 %pick.1 = bf16[3,256,1792]{2,1,0:T(8,128)(2,1)S(1)} custom-call(s32[1]{0:T(128)} %bitcast.me_ref, s32[256]{0:T(256)} %slots_ref.5, bf16[3,3,256,2048]{3,2,1,0:T(8,128)(2,1)} %own_ref.3), custom_call_target="tpu_custom_call" | custom-call | bytes 5505024 | tf_op jit(solution)/shard_map/pick/pallas_call | solution.py:89
  3.5 3.0 %collective-permute-start.2 = (bf16[3,256,1792]{2,1,0:T(8,128)(2,1)S(1)}, bf16[3,256,1792]{2,1,0:T(8,128)(2,1)S(1)}, u32[]{:S(2)}, u32[]{:S(2)}) collective-permute-start(bf16[3,256,1792]{2,1,0:T(8,128)(2,1)S(1)} %pick.1), channel_id=1, source_target_pairs={{2,1},{4,3},{6,5},{8,7},{10,9},{12,11},{14,13},{16,15},{18,17},{20... | collective-permute-start | bytes 8257544 | tf_op jit(solution)/shard_map/ppermute | solution.py:528
  6.5 0.8 %pair_counts.1 = (f32[16,16]{1,0:T(8,128)S(1)}, s32[8,128]{1,0:T(8,128)S(1)}) custom-call(s32[1]{0:T(128)} %bitcast.me_ref, s32[256]{0:T(256)S(1)} %copy-done.2, s32[2,6144]{1,0:T(2,128)S(1)} %bitcast.4, s32[4,6144]{1,0:T(4,128)S(1)} %bitcast.3), custom_call_target="tpu_custom_call" | custom-call | flops 4000000 | bytes 200000 | tf_op jit(solution)/shard_map/pair_counts/pallas_call | solution.py:155
  7.3 5.9 %edge_mix.1 = (bf16[3,512,1792]{2,1,0:T(8,128)(2,1)S(1)}, bf16[3,512,256]{2,1,0:T(8,128)(2,1)S(1)}, bf16[3,512,256]{2,1,0:T(8,128)(2,1)S(1)}) custom-call(s32[8,128]{1,0:T(8,128)S(1)} %get-tuple-element.25.meta_ref, f32[16,16]{1,0:T(8,128)S(1)} %get-tuple-element.26.counts_ref, bf16[3,3,256,2048]{3,2,1,0:T(8,128)(2,1)} %own_ref.3), custom_call_target="tpu_custom_call" | custom-call | flops 30000000 | bytes 10000000 | tf_op jit(solution)/shard_map/edge_mix/pallas_call | solution.py:232
  13.2 2.1 %collective-permute-done.partner_ref.partner_hbm = bf16[3,3,256,2048]{3,2,1,0:T(8,128)(2,1)} collective-permute-done((bf16[3,3,256,2048]{3,2,1,0:T(8,128)(2,1)}, bf16[3,3,256,2048]{3,2,1,0:T(8,128)(2,1)}, u32[]{:S(2)}, u32[]{:S(2)}) %collective-permute-start) | collective-permute-done | bytes 9437216 | tf_op jit(solution)/shard_map/ppermute | solution.py:529
  15.3 2.0 %pick_two.1 = (bf16[2,3,256,256]{3,2,1,0:T(8,128)(2,1)S(1)}, f32[8,128]{1,0:T(8,128)S(1)}) custom-call(s32[1]{0:T(128)} %bitcast.me_ref, s32[256]{0:T(256)} %slots_ref.5, bf16[3,3,256,2048]{3,2,1,0:T(8,128)(2,1)} %own_ref.3, bf16[3,3,256,2048]{3,2,1,0:T(8,128)(2,1)} %collective-permute-done.partner_ref.partner_hbm, ...), custom_call_target="tpu_custom_call" | custom-call | bytes 1572864 | tf_op jit(solution)/shard_map/pick_two/pallas_call | solution.py:89
  17.3 4.7 %collective-permute-start.1 = (bf16[2,3,256,256]{3,2,1,0:T(8,128)(2,1)S(1)}, bf16[2,3,256,256]{3,2,1,0:T(8,128)(2,1)S(1)}, u32[]{:S(2)}, u32[]{:S(2)}) collective-permute-start(bf16[2,3,256,256]{3,2,1,0:T(8,128)(2,1)S(1)} %get-tuple-element.32), channel_id=1, source_target_pairs={{2,1},{4,3},{6,5},{8,7},{10,9},{12,11},{14,13},{16,15},{18,17},{20... | collective-permute-start | bytes 2359304 | tf_op jit(solution)/shard_map/ppermute | solution.py:533
  22.0 13.9 %own_and_inner.1 = (f32[3,256,256]{2,1,0:T(8,128)S(1)}, f32[256,256]{1,0:T(8,128)S(1)}, f32[256,256]{1,0:T(8,128)S(1)}, bf16[3,512,1792]{2,1,0:T(8,128)(2,1)S(1)}, bf16[3,512,256]{2,1,0:T(8,128)(2,1)S(1)}) custom-call(s32[8,128]{1,0:T(8,128)S(1)} %get-tuple-element.25.meta_ref, f32[16,16]{1,0:T(8,128)S(1)} %get-tuple-element.26.counts_ref, ...), custom_call_target="tpu_custom_call" | custom-call | flops 13421772800 | bytes 16000000 | tf_op jit(solution)/shard_map/own_and_inner/pallas_call | solution.py:365
  36.0 6.1 %collective-permute-done.2.outer_ref = bf16[3,256,1792]{2,1,0:T(8,128)(2,1)S(1)} collective-permute-done((bf16[3,256,1792]{2,1,0:T(8,128)(2,1)S(1)}, bf16[3,256,1792]{2,1,0:T(8,128)(2,1)S(1)}, u32[]{:S(2)}, u32[]{:S(2)}) %collective-permute-start.2) | collective-permute-done | bytes 2752544 | tf_op jit(solution)/shard_map/ppermute | solution.py:528
  42.1 1.7 %outer_early.1 = (f32[256,256]{1,0:T(8,128)S(1)}, f32[256,256]{1,0:T(8,128)S(1)}) custom-call(bf16[3,512,1792]{2,1,0:T(8,128)(2,1)S(1)} %get-tuple-element.34.mix_ref, bf16[3,256,1792]{2,1,0:T(8,128)(2,1)S(1)} %collective-permute-done.2.outer_ref), custom_call_target="tpu_custom_call" | custom-call | flops 1409286144 | bytes 1000000 | tf_op jit(solution)/shard_map/outer_early/pallas_call | solution.py:408
  43.7 3.0 %collective-permute-start.4 = (f32[256,256]{1,0:T(8,128)S(1)}, f32[256,256]{1,0:T(8,128)S(1)}, u32[]{:S(2)}, u32[]{:S(2)}) collective-permute-start(f32[256,256]{1,0:T(8,128)S(1)} %get-tuple-element.42), channel_id=1, source_target_pairs={{2,1},{4,3},{6,5},{8,7},{10,9},{12,11},{14,13},{16,15},{18,17},{20... | collective-permute-start | bytes 786440 | tf_op jit(solution)/shard_map/ppermute | solution.py:537
  46.8 0.1 collective-permute-start.3
  46.9 1.6 %outer_adjacent.1.adj_in = f32[256,256]{1,0:T(8,128)S(1)} custom-call(bf16[3,512,1792]{2,1,0:T(8,128)(2,1)S(1)} %get-tuple-element.33.mix_ref, bf16[3,256,1792]{2,1,0:T(8,128)(2,1)S(1)} %collective-permute-done.2.outer_ref), custom_call_target="tpu_custom_call" | custom-call | flops 1409286144 | bytes 1000000 | tf_op jit(solution)/shard_map/outer_adjacent/pallas_call | solution.py:428
  48.5 2.0 %collective-permute-done.1.outer_ref = bf16[2,3,256,256]{3,2,1,0:T(8,128)(2,1)S(1)} collective-permute-done((bf16[2,3,256,256]{3,2,1,0:T(8,128)(2,1)S(1)}, bf16[2,3,256,256]{3,2,1,0:T(8,128)(2,1)S(1)}, u32[]{:S(2)}, u32[]{:S(2)}) %collective-permute-start.1) | collective-permute-done | bytes 786464 | tf_op jit(solution)/shard_map/ppermute | solution.py:533
  50.5 1.4 %outer_late.1 = (f32[256,256]{1,0:T(8,128)S(1)}, f32[256,256]{1,0:T(8,128)S(1)}, f32[128,256]{1,0:T(8,128)S(1)}, f32[128,256]{1,0:T(8,128)S(1)}) custom-call(s32[8,128]{1,0:T(8,128)S(1)} %get-tuple-element.25.meta_ref, bf16[3,512,256]{2,1,0:T(8,128)(2,1)S(1)} %get-tuple-element.30.adj_mix, bf16[3,512,256]{2,1,0:T(8,128)(2,1)S(1)} %get-tuple-element.31.sec_mix, ...), custom_call_target="tpu_custom_call" | custom-call | flops 603979776 | bytes 1000000 | tf_op jit(solution)/shard_map/outer_late/pallas_call | solution.py:458
  51.9 0.1 collective-permute-start.5
  52.0 0.5 collective-permute-start.6
  52.5 0.0 collective-permute-done.3.next_ref
  52.5 0.7 %settle.1 = (f32[3,256,256]{2,1,0:T(8,128)S(1)}, f32[8,256]{1,0:T(8,128)S(1)}) custom-call(s32[8,128]{1,0:T(8,128)S(1)} %get-tuple-element.25.meta_ref, f32[3,256,256]{2,1,0:T(8,128)S(1)} %get-tuple-element.29.sum_ref, f32[256,256]{1,0:T(8,128)S(1)} %get-tuple-element.37.adj_ref, f32[256,256]{1,0:T(8,128)S(1)} %get-tuple-element.38.sec_ref, ...), custom_call_target="tpu_custom_call" | custom-call | flops 200000 | bytes 2000000 | tf_op jit(solution)/shard_map/settle/pallas_call | solution.py:487
  53.2 2.4 %collective-permute-done.4.outer_ref = f32[256,256]{1,0:T(8,128)S(1)} collective-permute-done((f32[256,256]{1,0:T(8,128)S(1)}, f32[256,256]{1,0:T(8,128)S(1)}, u32[]{:S(2)}, u32[]{:S(2)}) %collective-permute-start.4) | collective-permute-done | bytes 262176 | tf_op jit(solution)/shard_map/ppermute | solution.py:537
  55.7 0.0 collective-permute-done.5.near_top
  55.7 0.0 collective-permute-done.6.near_low
  55.7 1.0 %finish.1 = f32[3,256,256]{2,1,0:T(8,128)} custom-call(f32[8,256]{1,0:T(8,128)S(1)} %get-tuple-element.40.place_ref, f32[3,256,256]{2,1,0:T(8,128)S(1)} %get-tuple-element.41.sum_ref, f32[256,256]{1,0:T(8,128)S(1)} %collective-permute-done.4.outer_ref, f32[128,256]{1,0:T(8,128)S(1)} %collective-permute-done.5.near_top, ...), custom_call_target="tpu_custom_call" | custom-call | flops 200000 | bytes 2000000 | tf_op jit(solution)/shard_map/finish/pallas_call | solution.py:511
  (6 shorter events, 0.0 us)
Async XLA Ops:
  0.0 15.3 %collective-permute-start = (bf16[3,3,256,2048]{3,2,1,0:T(8,128)(2,1)}, bf16[3,3,256,2048]{3,2,1,0:T(8,128)(2,1)}, u32[]{:S(2)}, u32[]{:S(2)}) collective-permute-start(bf16[3,3,256,2048]{3,2,1,0:T(8,128)(2,1)} %own_ref.3), channel_id=1, source_target_pairs={{0,1},{1,0},{2,3},{3,2},{4,5},{5,4},{6,7},{7,6},{8,9},{9,8},{10,11... | collective-permute-start | bytes 28311560 | tf_op jit(solution)/shard_map/ppermute | solution.py:529
  0.7 5.8 %copy-start = (s32[6144,4]{0,1:T(4,128)S(1)}, s32[6144,4]{0,1:T(4,128)}, u32[]{:S(2)}) copy-start(s32[6144,4]{0,1:T(4,128)} %param.7) | copy-start | bytes 294916
  0.7 5.8 %copy-start.1 = (s32[6144,2]{0,1:T(2,128)S(1)}, s32[6144,2]{0,1:T(2,128)}, u32[]{:S(2)}) copy-start(s32[6144,2]{0,1:T(2,128)} %param.6) | copy-start | bytes 147460
  0.7 5.8 %copy-start.2 = (s32[256]{0:T(256)S(1)}, s32[256]{0:T(256)}, u32[]{:S(2)}) copy-start(s32[256]{0:T(256)} %slots_ref.5) | copy-start | bytes 3076
  3.5 38.6 %collective-permute-start.2 = (bf16[3,256,1792]{2,1,0:T(8,128)(2,1)S(1)}, bf16[3,256,1792]{2,1,0:T(8,128)(2,1)S(1)}, u32[]{:S(2)}, u32[]{:S(2)}) collective-permute-start(bf16[3,256,1792]{2,1,0:T(8,128)(2,1)S(1)} %pick.1), channel_id=1, source_target_pairs={{2,1},{4,3},{6,5},{8,7},{10,9},{12,11},{14,13},{16,15},{18,17},{20... | collective-permute-start | bytes 8257544 | tf_op jit(solution)/shard_map/ppermute | solution.py:528
  17.3 33.2 %collective-permute-start.1 = (bf16[2,3,256,256]{3,2,1,0:T(8,128)(2,1)S(1)}, bf16[2,3,256,256]{3,2,1,0:T(8,128)(2,1)S(1)}, u32[]{:S(2)}, u32[]{:S(2)}) collective-permute-start(bf16[2,3,256,256]{3,2,1,0:T(8,128)(2,1)S(1)} %get-tuple-element.32), channel_id=1, source_target_pairs={{2,1},{4,3},{6,5},{8,7},{10,9},{12,11},{14,13},{16,15},{18,17},{20... | collective-permute-start | bytes 2359304 | tf_op jit(solution)/shard_map/ppermute | solution.py:533
  43.7 11.9 %collective-permute-start.4 = (f32[256,256]{1,0:T(8,128)S(1)}, f32[256,256]{1,0:T(8,128)S(1)}, u32[]{:S(2)}, u32[]{:S(2)}) collective-permute-start(f32[256,256]{1,0:T(8,128)S(1)} %get-tuple-element.42), channel_id=1, source_target_pairs={{2,1},{4,3},{6,5},{8,7},{10,9},{12,11},{14,13},{16,15},{18,17},{20... | collective-permute-start | bytes 786440 | tf_op jit(solution)/shard_map/ppermute | solution.py:537
  46.8 5.7 %collective-permute-start.3 = (f32[256,256]{1,0:T(8,128)S(1)}, f32[256,256]{1,0:T(8,128)S(1)}, u32[]{:S(2)}, u32[]{:S(2)}) collective-permute-start(f32[256,256]{1,0:T(8,128)S(1)} %get-tuple-element.39), channel_id=1, source_target_pairs={{0,1},{1,0},{2,3},{3,2},{4,5},{5,4},{6,7},{7,6},{8,9},{9,8},{10,11... | collective-permute-start | bytes 786440 | tf_op jit(solution)/shard_map/ppermute | solution.py:535
  51.9 3.8 %collective-permute-start.5 = (f32[128,256]{1,0:T(8,128)S(1)}, f32[128,256]{1,0:T(8,128)S(1)}, u32[]{:S(2)}, u32[]{:S(2)}) collective-permute-start(f32[128,256]{1,0:T(8,128)S(1)} %get-tuple-element.43), channel_id=1, source_target_pairs={{0,1},{1,0},{2,3},{3,2},{4,5},{5,4},{6,7},{7,6},{8,9},{9,8},{10,11... | collective-permute-start | bytes 393224 | tf_op jit(solution)/shard_map/ppermute | solution.py:540
  52.0 3.7 %collective-permute-start.6 = (f32[128,256]{1,0:T(8,128)S(1)}, f32[128,256]{1,0:T(8,128)S(1)}, u32[]{:S(2)}, u32[]{:S(2)}) collective-permute-start(f32[128,256]{1,0:T(8,128)S(1)} %get-tuple-element.44), channel_id=1, source_target_pairs={{0,1},{1,0},{2,3},{3,2},{4,5},{5,4},{6,7},{7,6},{8,9},{9,8},{10,11... | collective-permute-start | bytes 393224 | tf_op jit(solution)/shard_map/ppermute | solution.py:540

commit v4 on v3

--- a/solution.py
+++ b/solution.py
@@ -47,18 +47,7 @@
     live, _, even = layout(cap, me_ref[0], slots_ref)
     slot = jnp.where(even, 0, live - 1)
     width = out_ref.shape[-1]
-    part = own_ref.shape[2] // 4
-    run_copies(
-        [
-            (
-                own_ref.at[slot, k, pl.ds(q * part, part), pl.ds(0, width)],
-                out_ref.at[k, pl.ds(q * part, part)],
-            )
-            for k in range(3)
-            for q in range(4)
-        ],
-        sems,
-    )
+    run_copies([(own_ref.at[slot, k, :, pl.ds(0, width)], out_ref.at[k]) for k in range(3)], sems)
 
 
 def pick_two_kernel(cap, start, me_ref, slots_ref, own_ref, partner_ref, after, out_ref, token_ref, sems):
@@ -92,7 +81,7 @@
         in_specs=[smem, smem, pl.BlockSpec(memory_space=pltpu.HBM)]
         + [pl.BlockSpec(memory_space=pl.ANY)] * (len(blocks) - 1 + len(after)),
         out_specs=(pl.BlockSpec(memory_space=pltpu.VMEM),) * len(blocks),
-        scratch_shapes=[pltpu.SemaphoreType.DMA((12,))],
+        scratch_shapes=[pltpu.SemaphoreType.DMA((6,))],
         compiler_params=pltpu.CompilerParams(vmem_limit_bytes=LATE_LIMIT),
         name=name,
         cost_estimate=pl.CostEstimate(flops=0, bytes_accessed=moved, transcendentals=0),

time: 57 us -> 56.8 us (level)
  waiting for transfers between devices: 12.6 us -> 10.9 us
  Pallas kernels: 31.9 us -> 33.5 us
    pallas_call x1, Pallas kernels: 13.9 us -> 15.8 us  [main_part(): pl.pallas_call(main_kernel, in_specs=[smem, smem, hbm, free, free], out_s...]
    ppermute x1, waiting for transfers between devices: 6.07 us -> 4.27 us  [per_device(): outer_early = lax.ppermute(pick_early(me, block_slot, own), 'blk', to_outer)]
  transfers between devices with their start and end apart: 7 -> 7, of which waited for: 4 -> 4; matrix products, arithmetic and copies ran while one was open for 0% -> 0% of each run, Pallas kernels for 54% -> 58%
where the time goes in v4:
time: 56.8 us; the launch traced here: 56.5 us
  Pallas kernels  33.5 us (59%)
  starting transfers between devices  11.9 us (21%)
  waiting for transfers between devices  10.9 us (19%)
    pallas_call x1, Pallas kernels, main_part(): pl.pallas_call(main_kernel, in_specs=[smem, smem, hbm, free, free], out_s...  15.8 us
    pallas_call x1, Pallas kernels, edge_part(): pl.pallas_call(edge_kernel, in_specs=[smem, smem, pl.BlockSpec(memory_spa...  5.9 us
    pallas_call x2, Pallas kernels, pick_call(): pl.pallas_call(kernel, out_shape=(pltpu.VMEM(shape, blocks[0].dtype),) +...  4.59 us
    ppermute x1, starting transfers between devices, per_device(): outer_late = lax.ppermute(late_piece, 'blk', to_outer)  4.54 us
    ppermute x1, waiting for transfers between devices, per_device(): outer_early = lax.ppermute(pick_early(me, block_slot, own), 'blk', to_outer)  4.27 us
    ppermute x1, starting transfers between devices, per_device(): from_outer = lax.ppermute(outer_back, 'blk', to_outer)  3.02 us
    ppermute x1, starting transfers between devices, per_device(): outer_early = lax.ppermute(pick_early(me, block_slot, own), 'blk', to_outer)  3.02 us
    ppermute x1, waiting for transfers between devices, per_device(): from_outer = lax.ppermute(outer_back, 'blk', to_outer)  2.42 us
  transfers between devices with their start and end apart: 7, of which 4 were waited for; matrix products, arithmetic and copies ran while one was open for 0% of the time, Pallas kernels for 58%

profile of v4, /device:TPU:63, one launch (start us, length us, event | category | flops | bytes accessed | tf_op | source)
XLA Modules:
  0.0 56.5 jit_solution(12722002221446470980)
XLA Ops:
  0.0 0.7 %collective-permute-start = (bf16[3,3,256,2048]{3,2,1,0:T(8,128)(2,1)}, bf16[3,3,256,2048]{3,2,1,0:T(8,128)(2,1)}, u32[]{:S(2)}, u32[]{:S(2)}) collective-permute-start(bf16[3,3,256,2048]{3,2,1,0:T(8,128)(2,1)} %own_ref.3), channel_id=1, source_target_pairs={{0,1},{1,0},{2,3},{3,2},{4,5},{5,4},{6,7},{7,6},{8,9},{9,8},{10,11... | collective-permute-start | bytes 28311560 | tf_op jit(solution)/shard_map/ppermute | solution.py:518
  0.7 2.6 %pick.1 = bf16[3,256,1792]{2,1,0:T(8,128)(2,1)S(1)} custom-call(s32[1]{0:T(128)} %bitcast.me_ref, s32[256]{0:T(256)} %slots_ref.5, bf16[3,3,256,2048]{3,2,1,0:T(8,128)(2,1)} %own_ref.3), custom_call_target="tpu_custom_call" | custom-call | bytes 5505024 | tf_op jit(solution)/shard_map/pick/pallas_call | solution.py:78
  3.3 3.0 %collective-permute-start.2 = (bf16[3,256,1792]{2,1,0:T(8,128)(2,1)S(1)}, bf16[3,256,1792]{2,1,0:T(8,128)(2,1)S(1)}, u32[]{:S(2)}, u32[]{:S(2)}) collective-permute-start(bf16[3,256,1792]{2,1,0:T(8,128)(2,1)S(1)} %pick.1), channel_id=1, source_target_pairs={{2,1},{4,3},{6,5},{8,7},{10,9},{12,11},{14,13},{16,15},{18,17},{20... | collective-permute-start | bytes 8257544 | tf_op jit(solution)/shard_map/ppermute | solution.py:517
  6.4 0.8 %pair_counts.1 = (f32[16,16]{1,0:T(8,128)S(1)}, s32[8,128]{1,0:T(8,128)S(1)}) custom-call(s32[1]{0:T(128)} %bitcast.me_ref, s32[256]{0:T(256)S(1)} %copy-done.2, s32[2,6144]{1,0:T(2,128)S(1)} %bitcast.4, s32[4,6144]{1,0:T(4,128)S(1)} %bitcast.3), custom_call_target="tpu_custom_call" | custom-call | flops 4000000 | bytes 200000 | tf_op jit(solution)/shard_map/pair_counts/pallas_call | solution.py:144
  7.2 5.9 %edge_mix.1 = (bf16[3,512,1792]{2,1,0:T(8,128)(2,1)S(1)}, bf16[3,512,256]{2,1,0:T(8,128)(2,1)S(1)}, bf16[3,512,256]{2,1,0:T(8,128)(2,1)S(1)}) custom-call(s32[8,128]{1,0:T(8,128)S(1)} %get-tuple-element.25.meta_ref, f32[16,16]{1,0:T(8,128)S(1)} %get-tuple-element.26.counts_ref, bf16[3,3,256,2048]{3,2,1,0:T(8,128)(2,1)} %own_ref.3), custom_call_target="tpu_custom_call" | custom-call | flops 30000000 | bytes 10000000 | tf_op jit(solution)/shard_map/edge_mix/pallas_call | solution.py:221
  13.1 2.2 %collective-permute-done.partner_ref.partner_hbm = bf16[3,3,256,2048]{3,2,1,0:T(8,128)(2,1)} collective-permute-done((bf16[3,3,256,2048]{3,2,1,0:T(8,128)(2,1)}, bf16[3,3,256,2048]{3,2,1,0:T(8,128)(2,1)}, u32[]{:S(2)}, u32[]{:S(2)}) %collective-permute-start) | collective-permute-done | bytes 9437216 | tf_op jit(solution)/shard_map/ppermute | solution.py:518
  15.3 2.0 %pick_two.1 = (bf16[2,3,256,256]{3,2,1,0:T(8,128)(2,1)S(1)}, f32[8,128]{1,0:T(8,128)S(1)}) custom-call(s32[1]{0:T(128)} %bitcast.me_ref, s32[256]{0:T(256)} %slots_ref.5, bf16[3,3,256,2048]{3,2,1,0:T(8,128)(2,1)} %own_ref.3, bf16[3,3,256,2048]{3,2,1,0:T(8,128)(2,1)} %collective-permute-done.partner_ref.partner_hbm, ...), custom_call_target="tpu_custom_call" | custom-call | bytes 1572864 | tf_op jit(solution)/shard_map/pick_two/pallas_call | solution.py:78
  17.3 4.5 %collective-permute-start.1 = (bf16[2,3,256,256]{3,2,1,0:T(8,128)(2,1)S(1)}, bf16[2,3,256,256]{3,2,1,0:T(8,128)(2,1)S(1)}, u32[]{:S(2)}, u32[]{:S(2)}) collective-permute-start(bf16[2,3,256,256]{3,2,1,0:T(8,128)(2,1)S(1)} %get-tuple-element.32), channel_id=1, source_target_pairs={{2,1},{4,3},{6,5},{8,7},{10,9},{12,11},{14,13},{16,15},{18,17},{20... | collective-permute-start | bytes 2359304 | tf_op jit(solution)/shard_map/ppermute | solution.py:522
  21.8 15.8 %own_and_inner.1 = (f32[3,256,256]{2,1,0:T(8,128)S(1)}, f32[256,256]{1,0:T(8,128)S(1)}, f32[256,256]{1,0:T(8,128)S(1)}, bf16[3,512,1792]{2,1,0:T(8,128)(2,1)S(1)}, bf16[3,512,256]{2,1,0:T(8,128)(2,1)S(1)}) custom-call(s32[8,128]{1,0:T(8,128)S(1)} %get-tuple-element.25.meta_ref, f32[16,16]{1,0:T(8,128)S(1)} %get-tuple-element.26.counts_ref, ...), custom_call_target="tpu_custom_call" | custom-call | flops 13421772800 | bytes 16000000 | tf_op jit(solution)/shard_map/own_and_inner/pallas_call | solution.py:354
  37.6 4.3 %collective-permute-done.2.outer_ref = bf16[3,256,1792]{2,1,0:T(8,128)(2,1)S(1)} collective-permute-done((bf16[3,256,1792]{2,1,0:T(8,128)(2,1)S(1)}, bf16[3,256,1792]{2,1,0:T(8,128)(2,1)S(1)}, u32[]{:S(2)}, u32[]{:S(2)}) %collective-permute-start.2) | collective-permute-done | bytes 2752544 | tf_op jit(solution)/shard_map/ppermute | solution.py:517
  41.9 1.7 %outer_early.1 = (f32[256,256]{1,0:T(8,128)S(1)}, f32[256,256]{1,0:T(8,128)S(1)}) custom-call(bf16[3,512,1792]{2,1,0:T(8,128)(2,1)S(1)} %get-tuple-element.34.mix_ref, bf16[3,256,1792]{2,1,0:T(8,128)(2,1)S(1)} %collective-permute-done.2.outer_ref), custom_call_target="tpu_custom_call" | custom-call | flops 1409286144 | bytes 1000000 | tf_op jit(solution)/shard_map/outer_early/pallas_call | solution.py:397
  43.6 3.0 %collective-permute-start.4 = (f32[256,256]{1,0:T(8,128)S(1)}, f32[256,256]{1,0:T(8,128)S(1)}, u32[]{:S(2)}, u32[]{:S(2)}) collective-permute-start(f32[256,256]{1,0:T(8,128)S(1)} %get-tuple-element.42), channel_id=1, source_target_pairs={{2,1},{4,3},{6,5},{8,7},{10,9},{12,11},{14,13},{16,15},{18,17},{20... | collective-permute-start | bytes 786440 | tf_op jit(solution)/shard_map/ppermute | solution.py:526
  46.6 0.1 collective-permute-start.3
  46.7 1.6 %outer_adjacent.1.adj_in = f32[256,256]{1,0:T(8,128)S(1)} custom-call(bf16[3,512,1792]{2,1,0:T(8,128)(2,1)S(1)} %get-tuple-element.33.mix_ref, bf16[3,256,1792]{2,1,0:T(8,128)(2,1)S(1)} %collective-permute-done.2.outer_ref), custom_call_target="tpu_custom_call" | custom-call | flops 1409286144 | bytes 1000000 | tf_op jit(solution)/shard_map/outer_adjacent/pallas_call | solution.py:417
  48.3 2.0 %collective-permute-done.1.outer_ref = bf16[2,3,256,256]{3,2,1,0:T(8,128)(2,1)S(1)} collective-permute-done((bf16[2,3,256,256]{3,2,1,0:T(8,128)(2,1)S(1)}, bf16[2,3,256,256]{3,2,1,0:T(8,128)(2,1)S(1)}, u32[]{:S(2)}, u32[]{:S(2)}) %collective-permute-start.1) | collective-permute-done | bytes 786464 | tf_op jit(solution)/shard_map/ppermute | solution.py:522
  50.3 1.4 %outer_late.1 = (f32[256,256]{1,0:T(8,128)S(1)}, f32[256,256]{1,0:T(8,128)S(1)}, f32[128,256]{1,0:T(8,128)S(1)}, f32[128,256]{1,0:T(8,128)S(1)}) custom-call(s32[8,128]{1,0:T(8,128)S(1)} %get-tuple-element.25.meta_ref, bf16[3,512,256]{2,1,0:T(8,128)(2,1)S(1)} %get-tuple-element.30.adj_mix, bf16[3,512,256]{2,1,0:T(8,128)(2,1)S(1)} %get-tuple-element.31.sec_mix, ...), custom_call_target="tpu_custom_call" | custom-call | flops 603979776 | bytes 1000000 | tf_op jit(solution)/shard_map/outer_late/pallas_call | solution.py:447
  51.7 0.1 collective-permute-start.5
  51.8 0.5 collective-permute-start.6
  52.3 0.0 collective-permute-done.3.next_ref
  52.3 0.7 %settle.1 = (f32[3,256,256]{2,1,0:T(8,128)S(1)}, f32[8,256]{1,0:T(8,128)S(1)}) custom-call(s32[8,128]{1,0:T(8,128)S(1)} %get-tuple-element.25.meta_ref, f32[3,256,256]{2,1,0:T(8,128)S(1)} %get-tuple-element.29.sum_ref, f32[256,256]{1,0:T(8,128)S(1)} %get-tuple-element.37.adj_ref, f32[256,256]{1,0:T(8,128)S(1)} %get-tuple-element.38.sec_ref, ...), custom_call_target="tpu_custom_call" | custom-call | flops 200000 | bytes 2000000 | tf_op jit(solution)/shard_map/settle/pallas_call | solution.py:476
  53.1 2.4 %collective-permute-done.4.outer_ref = f32[256,256]{1,0:T(8,128)S(1)} collective-permute-done((f32[256,256]{1,0:T(8,128)S(1)}, f32[256,256]{1,0:T(8,128)S(1)}, u32[]{:S(2)}, u32[]{:S(2)}) %collective-permute-start.4) | collective-permute-done | bytes 262176 | tf_op jit(solution)/shard_map/ppermute | solution.py:526
  55.5 0.0 collective-permute-done.5.near_top
  55.5 0.0 collective-permute-done.6.near_low
  55.5 1.0 %finish.1 = f32[3,256,256]{2,1,0:T(8,128)} custom-call(f32[8,256]{1,0:T(8,128)S(1)} %get-tuple-element.40.place_ref, f32[3,256,256]{2,1,0:T(8,128)S(1)} %get-tuple-element.41.sum_ref, f32[256,256]{1,0:T(8,128)S(1)} %collective-permute-done.4.outer_ref, f32[128,256]{1,0:T(8,128)S(1)} %collective-permute-done.5.near_top, ...), custom_call_target="tpu_custom_call" | custom-call | flops 200000 | bytes 2000000 | tf_op jit(solution)/shard_map/finish/pallas_call | solution.py:500
  (6 shorter events, 0.0 us)
Async XLA Ops:
  0.0 15.3 %collective-permute-start = (bf16[3,3,256,2048]{3,2,1,0:T(8,128)(2,1)}, bf16[3,3,256,2048]{3,2,1,0:T(8,128)(2,1)}, u32[]{:S(2)}, u32[]{:S(2)}) collective-permute-start(bf16[3,3,256,2048]{3,2,1,0:T(8,128)(2,1)} %own_ref.3), channel_id=1, source_target_pairs={{0,1},{1,0},{2,3},{3,2},{4,5},{5,4},{6,7},{7,6},{8,9},{9,8},{10,11... | collective-permute-start | bytes 28311560 | tf_op jit(solution)/shard_map/ppermute | solution.py:518
  0.7 5.7 %copy-start = (s32[6144,4]{0,1:T(4,128)S(1)}, s32[6144,4]{0,1:T(4,128)}, u32[]{:S(2)}) copy-start(s32[6144,4]{0,1:T(4,128)} %param.7) | copy-start | bytes 294916
  0.7 5.7 %copy-start.1 = (s32[6144,2]{0,1:T(2,128)S(1)}, s32[6144,2]{0,1:T(2,128)}, u32[]{:S(2)}) copy-start(s32[6144,2]{0,1:T(2,128)} %param.6) | copy-start | bytes 147460
  0.7 5.7 %copy-start.2 = (s32[256]{0:T(256)S(1)}, s32[256]{0:T(256)}, u32[]{:S(2)}) copy-start(s32[256]{0:T(256)} %slots_ref.5) | copy-start | bytes 3076
  3.3 38.6 %collective-permute-start.2 = (bf16[3,256,1792]{2,1,0:T(8,128)(2,1)S(1)}, bf16[3,256,1792]{2,1,0:T(8,128)(2,1)S(1)}, u32[]{:S(2)}, u32[]{:S(2)}) collective-permute-start(bf16[3,256,1792]{2,1,0:T(8,128)(2,1)S(1)} %pick.1), channel_id=1, source_target_pairs={{2,1},{4,3},{6,5},{8,7},{10,9},{12,11},{14,13},{16,15},{18,17},{20... | collective-permute-start | bytes 8257544 | tf_op jit(solution)/shard_map/ppermute | solution.py:517
  17.3 33.1 %collective-permute-start.1 = (bf16[2,3,256,256]{3,2,1,0:T(8,128)(2,1)S(1)}, bf16[2,3,256,256]{3,2,1,0:T(8,128)(2,1)S(1)}, u32[]{:S(2)}, u32[]{:S(2)}) collective-permute-start(bf16[2,3,256,256]{3,2,1,0:T(8,128)(2,1)S(1)} %get-tuple-element.32), channel_id=1, source_target_pairs={{2,1},{4,3},{6,5},{8,7},{10,9},{12,11},{14,13},{16,15},{18,17},{20... | collective-permute-start | bytes 2359304 | tf_op jit(solution)/shard_map/ppermute | solution.py:522
  43.6 11.9 %collective-permute-start.4 = (f32[256,256]{1,0:T(8,128)S(1)}, f32[256,256]{1,0:T(8,128)S(1)}, u32[]{:S(2)}, u32[]{:S(2)}) collective-permute-start(f32[256,256]{1,0:T(8,128)S(1)} %get-tuple-element.42), channel_id=1, source_target_pairs={{2,1},{4,3},{6,5},{8,7},{10,9},{12,11},{14,13},{16,15},{18,17},{20... | collective-permute-start | bytes 786440 | tf_op jit(solution)/shard_map/ppermute | solution.py:526
  46.6 5.7 %collective-permute-start.3 = (f32[256,256]{1,0:T(8,128)S(1)}, f32[256,256]{1,0:T(8,128)S(1)}, u32[]{:S(2)}, u32[]{:S(2)}) collective-permute-start(f32[256,256]{1,0:T(8,128)S(1)} %get-tuple-element.39), channel_id=1, source_target_pairs={{0,1},{1,0},{2,3},{3,2},{4,5},{5,4},{6,7},{7,6},{8,9},{9,8},{10,11... | collective-permute-start | bytes 786440 | tf_op jit(solution)/shard_map/ppermute | solution.py:524
  51.7 3.8 %collective-permute-start.5 = (f32[128,256]{1,0:T(8,128)S(1)}, f32[128,256]{1,0:T(8,128)S(1)}, u32[]{:S(2)}, u32[]{:S(2)}) collective-permute-start(f32[128,256]{1,0:T(8,128)S(1)} %get-tuple-element.43), channel_id=1, source_target_pairs={{0,1},{1,0},{2,3},{3,2},{4,5},{5,4},{6,7},{7,6},{8,9},{9,8},{10,11... | collective-permute-start | bytes 393224 | tf_op jit(solution)/shard_map/ppermute | solution.py:529
  51.8 3.7 %collective-permute-start.6 = (f32[128,256]{1,0:T(8,128)S(1)}, f32[128,256]{1,0:T(8,128)S(1)}, u32[]{:S(2)}, u32[]{:S(2)}) collective-permute-start(f32[128,256]{1,0:T(8,128)S(1)} %get-tuple-element.44), channel_id=1, source_target_pairs={{0,1},{1,0},{2,3},{3,2},{4,5},{5,4},{6,7},{7,6},{8,9},{9,8},{10,11... | collective-permute-start | bytes 393224 | tf_op jit(solution)/shard_map/ppermute | solution.py:529
